TPU v7x, 128 devices: a whole 4x4x4 slice. The times are simulated.
128 devices in a mesh: fsdp: 32 (over z, x, core), ctx: 4 (over y).
Axes of the slice: x: 4, y: 4, z: 4, core: 2. Of those that a mesh axis runs over, the one named last changes fastest.
Arguments:
- block_input: bfloat16 [16384, 896], P(('fsdp', 'ctx')), may hold values from -6 to 6
- positions: int32 [16384], P(('fsdp', 'ctx')), may hold values from 0 to 1023, as said below
- first_gain: bfloat16 [896], P('fsdp'), may hold values from 0.099609375 to 1.8984375
- query_weight: bfloat16 [896, 896], P('fsdp'), may hold values from -0.1875 to 0.1875
- query_bias: bfloat16 [896], P('fsdp'), may hold values from -3 to 3
- key_weight: bfloat16 [896, 128], P('fsdp'), may hold values from -0.1875 to 0.1875
- value_weight: bfloat16 [896, 128], P('fsdp'), may hold values from -0.1875 to 0.1875
- value_bias: bfloat16 [128], P('fsdp'), may hold values from -3 to 3
- output_weight: bfloat16 [896, 896], P('fsdp'), may hold values from -0.5 to 0.5
- second_gain: bfloat16 [896], P('fsdp'), may hold values from 0.099609375 to 1.8984375
- gate_weight: bfloat16 [896, 4864], P('fsdp'), may hold values from -0.1875 to 0.1875
- up_weight: bfloat16 [896, 4864], P('fsdp'), may hold values from -0.1875 to 0.1875
- down_weight: bfloat16 [4864, 896], P('fsdp'), may hold values from -0.078125 to 0.078125
- cotangent: bfloat16 [16384, 896], P(('fsdp', 'ctx')), may hold values from -6 to 6
Outputs:
- block_output: bfloat16 [16384, 896], P(('fsdp', 'ctx'))
- grad_input: bfloat16 [16384, 896], P(('fsdp', 'ctx'))
- grad_first_gain: float32 [896], P(('fsdp', 'ctx'))
- grad_query_weight: float32 [896, 896], P(('fsdp', 'ctx'))
- grad_query_bias: float32 [896], P(('fsdp', 'ctx'))
- grad_key_weight: float32 [896, 128], P(('fsdp', 'ctx'))
- grad_value_weight: float32 [896, 128], P(('fsdp', 'ctx'))
- grad_value_bias: float32 [128], P(('fsdp', 'ctx'))
- grad_output_weight: float32 [896, 896], P(('fsdp', 'ctx'))
- grad_second_gain: float32 [896], P(('fsdp', 'ctx'))
- grad_gate_weight: float32 [896, 4864], P(('fsdp', 'ctx'))
- grad_up_weight: float32 [896, 4864], P(('fsdp', 'ctx'))
- grad_down_weight: float32 [4864, 896], P(('fsdp', 'ctx'))
Inputs may be any that keep to these rules, and one draw needn't show every extreme that they name: positions count up by one from 0 along each sequence, a token with position 0 begins a new sequence, the first token has position 0, no sequence is longer than 1024 tokens and one has exactly 1024.
All inputs are finite; a program needn't handle non-finite values.
Results may differ from a plain program's by a relative error of at most 0.018.
Values may be sent and summed in bfloat16 or wider, within the bound.
A program may use at most 192 MiB of HBM per device.

v0:
```python
import functools
import math

import jax
import jax.numpy as jnp
from jax import lax
from jax.experimental import pallas as pl
from jax.experimental.pallas import tpu as pltpu
from jax.sharding import PartitionSpec as P

D = 896
HEADS = 14
KV_HEADS = 2
HEAD_SIZE = 64
FF = 4864
SEQ = 1024
TOK = 128
REACH = 8
DP = 1024
UN = 38
UP = 48
UC = 32 * UP
AW = 2048

EPSILON = 1e-06
ROTARY_BASE = 1000000.0
MESH = pl.DeviceIdType.MESH
BF = jnp.bfloat16
F32 = jnp.float32
ANY = pl.BlockSpec(memory_space=pl.ANY)
VMEM = pl.BlockSpec(memory_space=pltpu.VMEM)


def place():
    f = lax.axis_index("fsdp")
    return f // 8, (f // 2) % 4, f % 2, lax.axis_index("ctx")


def plus(i, d):
    return lax.rem(i + d, 4)


def device(z, x, k, c):
    return ((z * 4 + x) * 2 + k, c)


def greet(targets):
    barrier = pltpu.get_barrier_semaphore()
    for t in targets:
        pl.semaphore_signal(barrier, inc=1, device_id=t, device_id_type=MESH)
    pl.semaphore_wait(barrier, len(targets))


class Copies:
    def __init__(self, send, recv):
        self.send, self.recv, self.count, self.all = send, recv, 0, []

    def go(self, src, dst, target):
        n = self.count
        self.count += 1
        copy = pltpu.make_async_remote_copy(
            src_ref=src,
            dst_ref=dst,
            send_sem=self.send.at[n],
            recv_sem=self.recv.at[n],
            device_id=target,
            device_id_type=MESH,
        )
        copy.start()
        self.all.append(copy)
        return copy

    def finish(self):
        for copy in self.all:
            copy.wait_send()


class RingGather:
    def __init__(self, cp, part, own, p, up, down):
        self.cp, self.part, self.p, self.up, self.down = cp, part, p, up, down
        self.up0 = cp.go(own(0), part(p, 0), up)
        self.down1 = cp.go(own(1), part(p, 1), down)
        self.up1 = cp.go(own(1), part(p, 1), up)
        self.down0 = cp.go(own(0), part(p, 0), down)

    def forward(self):
        self.up0.wait_recv()
        ref = self.part(plus(self.p, 3), 0)
        self.far0 = self.cp.go(ref, ref, self.up)
        self.down1.wait_recv()
        ref = self.part(plus(self.p, 1), 1)
        self.far1 = self.cp.go(ref, ref, self.down)

    def near(self):
        self.up1.wait_recv()
        self.down0.wait_recv()

    def far(self):
        self.far0.wait_recv()
        self.far1.wait_recv()


class RingScatter:
    def __init__(self, cp, send, add, p, up, down, far, near):
        self.cp, self.send, self.add, self.p, self.up, self.down = cp, send, add, p, up, down
        self.far, self.near = far, near
        self.far0 = cp.go(send(plus(p, 2), 0), far[0], up)
        self.far1 = cp.go(send(plus(p, 2), 1), far[1], down)

    def plain(self):
        self.up1 = self.cp.go(self.send(plus(self.p, 1), 1), self.near[0](1), self.up)
        self.down0 = self.cp.go(self.send(plus(self.p, 3), 0), self.near[1](0), self.down)

    def forward(self):
        self.far0.wait_recv()
        ref = self.add(plus(self.p, 1), 0, self.far[0])
        self.up0 = self.cp.go(ref, self.near[0](0), self.up)
        self.far1.wait_recv()
        ref = self.add(plus(self.p, 3), 1, self.far[1])
        self.down1 = self.cp.go(ref, self.near[1](1), self.down)

    def finish(self):
        for copy in (self.up1, self.down0, self.up0, self.down1):
            copy.wait_recv()


def halves(rows):
    first = rows // 2 // 16 * 16
    return (pl.ds(0, first), pl.ds(first, rows - first))


PIECES = ((0, 0, 0, D, UP), (2, 0, 0, 768, 32), (1, 1, 0, UC, 32), (2, 1, 768, 768, 32))
FFN = ((UP, D), (32, UC), (32, UC))


def start_line(cp, spot, refs, own):
    z, x, k, c, zs, xs = spot
    rings = []
    for n, way, first, count, rows in PIECES:
        cut, cols = halves(rows), pl.ds(first, count)

        def part(p, h, n=n, way=way, cut=cut, cols=cols):
            at = (z, p, k, cut[h], cols) if way else (p, x, k, cut[h], cols)
            return refs[n].at[at]

        def mine(h, n=n, cut=cut, cols=cols):
            return own[n].at[cut[h], cols]

        rings.append(RingGather(cp, part, mine, x if way else z, *(xs if way else zs)))
    return rings


def start_plane(cp, spot, refs):
    z, x, k, c, zs, xs = spot
    rings = []
    for n, way, first, count, rows in PIECES:
        cols = pl.ds(first, count)

        def part(p, h, n=n, way=way, cols=cols):
            some = pl.ds(2 * h, 2)
            at = (p, some, k, slice(None), cols) if way else (some, p, k, slice(None), cols)
            return refs[n].at[at]

        p = z if way else x
        rings.append(RingGather(cp, part, functools.partial(part, p), p, *(zs if way else xs)))
    return rings


def gather_kernel(q, kw, v, o, down, gate, up, vec, t, *refs):
    ao, oo, do, go, uo, to = refs[:6]
    wq, wk, wv, wo, wd, wg, wu, units, own_a, own_o, own_d, own_g, own_u = refs[6:19]
    send, recv, load, loc = refs[19:]
    z, x, k, c = place()
    f = lax.axis_index("fsdp")
    zs = [device(plus(z, i), x, k, c) for i in (1, 3)]
    xs = [device(z, plus(x, i), k, c) for i in (1, 3)]
    ys = [device(z, x, k, plus(c, i)) for i in (1, 3)]
    sibling = device(z, x, 1 - k, c)
    loads = [
        pltpu.make_async_copy(src, dst, load.at[i])
        for i, (src, dst) in enumerate(
            ((q, wq), (kw, wk), (v, wv), (o, wo), (gate, wg), (up, wu), (down, wd))
        )
    ]
    for copy in loads:
        copy.start()
    token_copy = pltpu.make_async_copy(t, to.at[c], loc.at[5])
    token_copy.start()
    for n, device_id in enumerate(zs + xs + ys + [sibling]):
        pl.semaphore_signal(
            pltpu.get_barrier_semaphore(), inc=1, device_id=device_id, device_id_type=MESH
        )

    def iota(shape, axis):
        return lax.broadcasted_iota(jnp.int32, shape, axis)

    def where(flags):
        return flags.astype(F32).astype(BF)

    i = iota((32, 28), 1)
    spread = where(i + i // 7 == iota((32, 28), 0))
    row = iota((32, 1), 0)
    i, j = iota((88, 1152), 0), iota((88, 1152), 1)
    place_at = jnp.where(i < 28, 28 * f + i, jnp.where(i < 32, 1024 + 4 * f + i - 28, -1))
    extra = dot(vec[...], where(place_at == j))
    extra = jnp.where(row == 7, extra, 0.0)
    for copy in loads[:3]:
        copy.wait()
    own_a[:, :896] = (dot(spread, wq[...]) + extra[:, :896]).astype(BF)
    own_a[:, 896:1024] = dot(spread, wk[...]).astype(BF)
    own_a[:, 1024:] = (dot(spread, wv[...]) + extra[:, 1024:]).astype(BF)
    i, j = iota((88, D), 0), iota((88, D), 1)
    one = dot(vec[...], where((i >= 32) & (i < 60) & (28 * f + i - 32 == j)))
    two = dot(vec[...], where((i >= 60) & (28 * f + i - 60 == j)))
    loads[3].wait()
    own_o[...] = (
        dot(spread, wo[...]) + jnp.where(row == 7, one, 0.0) + jnp.where(row == 15, two, 0.0)
    ).astype(BF)

    pl.semaphore_wait(pltpu.get_barrier_semaphore(), 7)
    cp = Copies(send, recv)
    ways = (0, 1)
    own, outs = (own_a, own_o), (ao, oo)
    local = []

    def keep(src, out):
        copy = pltpu.make_async_copy(src, out.at[z, x, k], loc.at[len(local)])
        copy.start()
        local.append(copy)

    first, second, third = [], [], []
    cut = halves(32)
    for m in range(2):

        def part(p, h, m=m):
            return outs[m].at[z, p, k, cut[h]] if ways[m] else outs[m].at[p, x, k, cut[h]]

        def mine(h, m=m):
            return own[m].at[cut[h]]

        first.append(RingGather(cp, part, mine, x if ways[m] else z, *(xs if ways[m] else zs)))
        keep(own[m], outs[m])
    rows = halves(t.shape[0])
    tokens = RingGather(cp, lambda p, h: to.at[p, rows[h]], lambda h: t.at[rows[h]], c, *ys)

    loads[6].wait()
    i, j = iota((UP, 152), 0), iota((UP, 152), 1)
    own_d[...] = dot(where(jnp.where(i < UN, i + UN * c, -1) == j), wd[...]).astype(BF)
    j = iota((1, 16 * UP), 1)
    wanted = jnp.where(j % UP < UN, (j // UP) * 152 + j % UP, -1000) + UN * c
    for r in range(19):
        units[r * 128 : (r + 1) * 128] = where(iota((128, 16 * UP), 0) + r * 128 == wanted)
    for m in range(2):
        first[m].forward()
    for copy, src, out in ((loads[4], wg, own_g), (loads[5], wu, own_u)):
        copy.wait()
        wide = dot(spread, src[...]).astype(BF)
        for h in range(2):
            some = dot(wide[:, h * 2432 : (h + 1) * 2432], units[...])
            out[:, h * 768 : (h + 1) * 768] = some.astype(BF)
    for m in range(2):
        first[m].near()
        first[m].far()
        local[m].wait()

        def part(p, h, m=m):
            some = pl.ds(2 * h, 2)
            return outs[m].at[p, some, k] if ways[m] else outs[m].at[some, p, k]

        p = z if ways[m] else x
        second.append(
            RingGather(cp, part, functools.partial(part, p), p, *(zs if ways[m] else xs))
        )
    line = start_line(cp, (z, x, k, c, zs, xs), (do, go, uo), (own_d, own_g, own_u))
    for src, out in ((own_d, do), (own_g, go), (own_u, uo)):
        keep(src, out)

    def pass_on(m, i):
        p = plus(z if ways[m] else x, i)
        ref = outs[m].at[p, :, k] if ways[m] else outs[m].at[:, p, k]
        third.append(cp.go(ref, ref, sibling))

    for m in range(2):
        pass_on(m, 0)
    for m in range(2):
        second[m].forward()
    tokens.forward()
    for ring in line:
        ring.forward()
    for m in range(2):
        second[m].near()
        pass_on(m, 1)
        pass_on(m, 3)
    for m in range(2):
        second[m].far()
        pass_on(m, 2)
    for ring in line + [tokens]:
        ring.near()
        ring.far()
    token_copy.wait()
    for copy in local[2:]:
        copy.wait()
    for copy in third:
        copy.wait_recv()
    cp.finish()


def gather(q, kw, v, o, down, gate, up, vec, t):
    def out(rows, columns):
        return jax.ShapeDtypeStruct((4, 4, 2, rows, columns), BF)

    weights = (q, kw, v, o, down, gate, up)
    packed = ((32, 1152), (32, D)) + FFN
    count = 16 * 2 + 6 + 6 * len(PIECES)
    return pl.pallas_call(
        gather_kernel,
        out_shape=[out(*p) for p in packed] + [jax.ShapeDtypeStruct((4,) + t.shape, BF)],
        in_specs=[ANY] * 7 + [VMEM, ANY],
        out_specs=[ANY] * 6,
        scratch_shapes=[pltpu.VMEM(w.shape, BF) for w in weights]
        + [pltpu.VMEM((2432, 16 * UP), BF)]
        + [pltpu.VMEM(p, BF) for p in packed]
        + [
            pltpu.SemaphoreType.DMA((count,)),
            pltpu.SemaphoreType.DMA((count,)),
            pltpu.SemaphoreType.DMA((7,)),
            pltpu.SemaphoreType.DMA((6,)),
        ],
        compiler_params=pltpu.CompilerParams(
            collective_id=0, has_side_effects=True, vmem_limit_bytes=40 * 1024 * 1024
        ),
        name="gather_weights",
    )(*weights, vec, t)


def stretch_device(i):
    i = lax.rem(i + 128, 128)
    return (i // 4, lax.rem(i, 4))


def iota(shape, axis):
    return lax.broadcasted_iota(jnp.int32, shape, axis)


def head_move(head, scale):
    i, j = iota((128, 128), 0), iota((128, 128), 1)
    half, group = head % 2, head // (HEADS // KV_HEADS)
    hit = (i // 64 == half) & (j // 64 == group) & (i % 64 == j % 64)
    return (hit.astype(F32) * scale).astype(BF)


def spread_heads(src, out, scale):
    for pair in range(HEADS // 2):
        tile = src[:, pair * 128 : (pair + 1) * 128]
        for head in (2 * pair, 2 * pair + 1):
            out[head] = dot(tile, head_move(head, scale)).astype(BF)


def join_heads(src, out):
    for pair in range(HEADS // 2):
        total = 0.0
        for head in (2 * pair, 2 * pair + 1):
            total = total + dot_t(src[head], head_move(head, 1.0))
        out[:, pair * 128 : (pair + 1) * 128] = total.astype(BF)


def seen_mask(first):
    key = iota((TOK, (REACH + 1) * TOK), 1)
    query = REACH * TOK + iota((TOK, 1), 0)
    return (key >= first[...]) & (key <= query)


def window_kernel(q, kv, first, d_in, g_in, u_in, out, att, logs, do, go, uo, qs, os, send, recv):
    me = lax.axis_index("fsdp") * 4 + lax.axis_index("ctx")
    z, x, k, c = place()
    zs = [device(plus(z, i), x, k, c) for i in (1, 3)]
    xs = [device(z, plus(x, i), k, c) for i in (1, 3)]
    greet([stretch_device(me - o) for o in range(1, REACH + 1)] + zs + xs)
    cp = Copies(send, recv)
    copies = [
        cp.go(kv, out.at[REACH - o], stretch_device(me + o)) for o in range(REACH, 0, -1)
    ]
    plane = start_plane(cp, (z, x, k, c, zs, xs), (do, go, uo))
    out[REACH] = kv[...]
    spread_heads(q, qs, 1.0 / math.sqrt(HEAD_SIZE))
    logs[...] = jnp.zeros(logs.shape, F32)
    for copy in copies:
        copy.wait_recv()
    for ring in plane:
        ring.forward()

    def one(head, carry):
        keys = out[:, :, :128].reshape((REACH + 1) * TOK, 128)
        values = out[:, :, 128:].reshape((REACH + 1) * TOK, 128)
        scores = jnp.where(seen_mask(first), dot_t(qs[head], keys), -jnp.inf)
        top = jnp.max(scores, axis=1, keepdims=True)
        weights = jnp.exp(scores - top)
        total = jnp.sum(weights, axis=1, keepdims=True)
        os[head] = dot((weights * (1.0 / total)).astype(BF), values).astype(BF)
        logs[...] += jnp.where(iota((TOK, 128), 1) == head, top + jnp.log(total), 0.0)
        return carry

    lax.fori_loop(0, HEADS, one, 0)
    join_heads(os, att)
    for ring in plane:
        ring.near()
        ring.far()
    cp.finish()


def window(q, kv, first, weights):
    count = REACH + 6 * len(PIECES)
    return pl.pallas_call(
        window_kernel,
        out_shape=[
            jax.ShapeDtypeStruct((REACH + 1,) + kv.shape, BF),
            jax.ShapeDtypeStruct(q.shape, BF),
            jax.ShapeDtypeStruct((TOK, 128), F32),
        ]
        + [jax.ShapeDtypeStruct(w.shape, BF) for w in weights],
        in_specs=[VMEM] * 3 + [ANY] * 3,
        out_specs=[VMEM] * 3 + [ANY] * 3,
        input_output_aliases={3: 3, 4: 4, 5: 5},
        scratch_shapes=[
            pltpu.VMEM((HEADS, TOK, 128), BF),
            pltpu.VMEM((HEADS, TOK, 128), BF),
            pltpu.SemaphoreType.DMA((count,)),
            pltpu.SemaphoreType.DMA((count,)),
        ],
        compiler_params=pltpu.CompilerParams(
            collective_id=1, has_side_effects=True, vmem_limit_bytes=48 * 1024 * 1024
        ),
        name="attention_forward",
    )(q, kv, first, *weights)


def back_kernel(q, grad, att, logs, seen, first, turn, *refs):
    n = len(PIECES)

    def take(count):
        nonlocal refs
        head, refs = refs[:count], refs[count:]
        return head

    ins, (out,), sums = take(n), take(1), take(n)
    own, far, near = take(n), take(n), take(n)
    qs, gs, os, grad_keys, grad_values, parts, got, send, recv, loc = refs
    me = lax.axis_index("fsdp") * 4 + lax.axis_index("ctx")
    z, x, k, c = place()
    zs = [device(plus(z, i), x, k, c) for i in (1, 3)]
    xs = [device(z, plus(x, i), k, c) for i in (1, 3)]
    loads = []
    for m in range(n):
        loads.append(pltpu.make_async_copy(ins[m], own[m], loc.at[m]))
        loads[m].start()
    greet([stretch_device(me + o) for o in range(1, REACH + 1)] + zs + xs)
    cp = Copies(send, recv)
    rings = []
    for m in range(n):
        way = PIECES[m][1]
        loads[m].wait()
        rings.append(
            RingScatter(
                cp,
                functools.partial(half_of, own[m], way),
                functools.partial(add_half, own[m], way),
                z if way else x,
                *(zs if way else xs),
                (far[m].at[0], far[m].at[1]),
                (
                    lambda h, m=m: near[m].at[0, pl.ds(2 * h, 2)],
                    lambda h, m=m: near[m].at[1, pl.ds(2 * h, 2)],
                ),
            )
        )
        rings[m].plain()
    spread_heads(q, qs, 1.0 / math.sqrt(HEAD_SIZE))
    spread_heads(grad, gs, 1.0)
    spread_heads(att, os, 1.0)
    rows = (REACH + 1) * TOK
    grad_keys[...] = jnp.zeros((rows, 128), F32)
    grad_values[...] = jnp.zeros((rows, 128), F32)

    def turned(values):
        low = iota(values.shape, 1) % 64 < 32
        other = jnp.where(low, pltpu.roll(values, 96, 1), pltpu.roll(values, 32, 1))
        return values * turn[0] + other * turn[1]

    def one(head, carry):
        keys = seen[:, :, :128].reshape(rows, 128)
        values = seen[:, :, 128:].reshape(rows, 128)
        here = iota((TOK, 128), 1) == head
        log_total = jnp.sum(jnp.where(here, logs[...], 0.0), axis=1, keepdims=True)
        delta = jnp.sum(
            gs[head].astype(F32) * os[head].astype(F32), axis=1, keepdims=True
        )
        scores = jnp.where(seen_mask(first), dot_t(qs[head], keys), -jnp.inf)
        probability = jnp.exp(scores - log_total)
        grad_scores = (probability * (dot_t(gs[head], values) - delta)).astype(BF)
        grad_values[...] += t_dot(probability.astype(BF), gs[head])
        grad_keys[...] += t_dot(grad_scores, qs[head])
        grad_query = dot(grad_scores, keys) * (1.0 / math.sqrt(HEAD_SIZE))
        os[head] = turned(grad_query).astype(BF)
        return carry

    lax.fori_loop(0, HEADS // 2, one, 0)
    for m in range(n):
        rings[m].forward()
    lax.fori_loop(HEADS // 2, HEADS, one, 0)
    parts[:, :, :128] = grad_keys[: REACH * TOK].astype(BF).reshape(REACH, TOK, 128)
    parts[:, :, 128:] = grad_values[: REACH * TOK].astype(BF).reshape(REACH, TOK, 128)
    copies = [
        cp.go(parts.at[REACH - o], got.at[o - 1], stretch_device(me - o))
        for o in range(REACH, 0, -1)
    ]
    join_heads(os, out)
    for m in range(n):
        rings[m].finish()
        sum_line(own[m], near[m], sums[m], PIECES[m][1], z if PIECES[m][1] else x)
    for copy in copies:
        copy.wait_recv()
    total_keys, total_values = grad_keys[REACH * TOK :], grad_values[REACH * TOK :]
    for o in range(REACH):
        total_keys = total_keys + got[o, :, :128].astype(F32)
        total_values = total_values + got[o, :, 128:].astype(F32)
    out[:, 896:1024] = turned(total_keys).astype(BF)
    out[:, 1024:] = total_values.astype(BF)
    cp.finish()


def half_of(ref, way, p, h):
    some = pl.ds(2 * h, 2)
    return ref.at[p, some] if way else ref.at[some, p]


def add_half(ref, way, p, h, got):
    def one(j, carry):
        at = (p, 2 * h + j) if way else (2 * h + j, p)
        ref[at] = (ref[at].astype(F32) + got[j].astype(F32)).astype(BF)
        return carry

    lax.fori_loop(0, 2, one, 0)
    return half_of(ref, way, p, h)


def sum_line(own, near, out, way, p):
    def one(j, carry):
        at = (p, j) if way else (j, p)
        total = own[at].astype(F32) + near[0, j].astype(F32)
        out[j] = (total + near[1, j].astype(F32)).astype(BF)
        return carry

    lax.fori_loop(0, 4, one, 0)


def back(q, grad, att, logs, seen, first, turn, arrays):
    n = len(PIECES)
    shapes = [s.shape[2:] for s in arrays]
    count = REACH + 6 * n
    rows = (REACH + 1) * TOK
    return pl.pallas_call(
        back_kernel,
        out_shape=[jax.ShapeDtypeStruct((TOK, 1152), BF)]
        + [jax.ShapeDtypeStruct((4,) + s, BF) for s in shapes],
        in_specs=[VMEM] * 7 + [ANY] * n,
        out_specs=[VMEM] * (n + 1),
        scratch_shapes=[pltpu.VMEM((4, 4) + s, BF) for s in shapes]
        + [pltpu.VMEM((2, 2) + s, BF) for s in shapes]
        + [pltpu.VMEM((2, 4) + s, BF) for s in shapes]
        + [pltpu.VMEM((HEADS, TOK, 128), BF)] * 3
        + [pltpu.VMEM((rows, 128), F32)] * 2
        + [pltpu.VMEM((REACH, TOK, 256), BF)] * 2
        + [
            pltpu.SemaphoreType.DMA((count,)),
            pltpu.SemaphoreType.DMA((count,)),
            pltpu.SemaphoreType.DMA((n,)),
        ],
        compiler_params=pltpu.CompilerParams(
            collective_id=2, has_side_effects=True, vmem_limit_bytes=48 * 1024 * 1024
        ),
        name="attention_backward",
    )(q, grad, att, logs, seen, first, turn, *arrays)


def tokens_kernel(t, d_in, g_in, u_in, out, do, go, uo, send, recv):
    z, x, k, c = place()
    ys = [device(z, x, k, plus(c, i)) for i in (1, 3)]
    sibling = device(z, x, 1 - k, c)
    greet(ys + [sibling])
    cp = Copies(send, recv)
    rows = halves(t.shape[0])
    ring = RingGather(cp, lambda p, h: out.at[p, rows[h]], lambda h: t.at[rows[h]], c, *ys)
    copies = []
    for ref in (go, uo, do):
        copies.append(cp.go(ref.at[:, :, k], ref.at[:, :, k], sibling))
    out[c] = t[...]
    ring.forward()
    ring.near()
    ring.far()
    for copy in copies:
        copy.wait_recv()
    cp.finish()


def tokens_gather(t, weights):
    return pl.pallas_call(
        tokens_kernel,
        out_shape=[jax.ShapeDtypeStruct((4,) + t.shape, BF)]
        + [jax.ShapeDtypeStruct(w.shape, BF) for w in weights],
        in_specs=[VMEM] + [ANY] * 3,
        out_specs=[VMEM] + [ANY] * 3,
        input_output_aliases={1: 1, 2: 2, 3: 3},
        scratch_shapes=[pltpu.SemaphoreType.DMA((9,)), pltpu.SemaphoreType.DMA((9,))],
        compiler_params=pltpu.CompilerParams(collective_id=3, has_side_effects=True),
        name="gather_tokens",
    )(t, *weights)


def tokens_ring(cp, t, acc, far, near, c, ys):
    rows = halves(t.shape[1])

    def send(p, h):
        return t.at[p, rows[h]]

    def add(p, h, got):
        acc[h] = (t[p, rows[h]].astype(F32) + got[...].astype(F32)).astype(BF)
        return acc.at[h]

    return RingScatter(
        cp,
        send,
        add,
        c,
        *ys,
        (far.at[0], far.at[1]),
        (lambda h: near.at[0, rows[h]], lambda h: near.at[1, rows[h]]),
    )


def tokens_scratch(rows):
    half = (2, rows[0] // 2, rows[1])
    return [pltpu.VMEM(half, BF), pltpu.VMEM(half, BF), pltpu.VMEM((2,) + rows, BF)]


def tokens_sum_kernel(t, hidden, cot, mid, gg, gu, wd, out, part, *refs):
    n = len(PIECES)

    def take(count):
        nonlocal refs
        head, refs = refs[:count], refs[count:]
        return head

    sums, full, got = take(n), take(3), take(n)
    acc, far, near, send, recv = refs
    z, x, k, c = place()
    ys = [device(z, x, k, plus(c, i)) for i in (1, 3)]
    sibling = device(z, x, 1 - k, c)
    greet(ys + [sibling])
    cp = Copies(send, recv)
    ring = tokens_ring(cp, t, acc, far, near, c, ys)
    ring.plain()
    firsts = {}

    def product(m, lhs, rhs):
        rows = lhs.shape[1] // 4
        shape = (4, 2) + full[m].shape[3:]

        def one(i, carry):
            columns = pl.ds(pl.multiple_of(i * rows, 128), rows)
            full[m][i] = t_dot(lhs[:, columns], rhs[...]).astype(BF).reshape(shape)
            return carry

        lax.fori_loop(0, 4, one, 0)
        for j in range(n):
            a, _, first, count, _ = PIECES[j]
            if a == m:
                src = full[m].at[:, :, 1 - k, :, pl.ds(first, count)]
                firsts[j] = cp.go(src, got[j], sibling)

    product(0, hidden, cot)
    ring.forward()
    product(1, mid, gg)
    product(2, mid, gu)
    ring.finish()
    out[...] = t[c].astype(F32) + near[0].astype(F32) + near[1].astype(F32)

    def down(i, carry):
        rows = pl.ds(pl.multiple_of(i * TOK, TOK), TOK)
        part[i] = dot(hidden[rows], wd[...]).astype(BF)
        return carry

    lax.fori_loop(0, 4, down, 0)
    for j in (0, 2, 1, 3):
        a, _, first, count, _ = PIECES[j]
        firsts[j].wait_recv()

        def add(i, carry, j=j, a=a, first=first, count=count):
            at = (i // 4, i % 4)
            mine = full[a][at + (k, slice(None), slice(first, first + count))]
            sums[j][at] = (mine.astype(F32) + got[j][at].astype(F32)).astype(BF)
            return carry

        lax.fori_loop(0, 16, add, 0)
    cp.finish()


def tokens_sum(t, hidden, cot, mid, gg, gu, wd):
    rows = t.shape[1:]
    n = len(PIECES)
    shapes = [(p[4], p[3]) for p in PIECES]
    return pl.pallas_call(
        tokens_sum_kernel,
        out_shape=[jax.ShapeDtypeStruct(rows, F32), jax.ShapeDtypeStruct(t.shape, BF)]
        + [jax.ShapeDtypeStruct((4, 4) + s, BF) for s in shapes],
        in_specs=[VMEM] * 7,
        out_specs=[VMEM] * (n + 2),
        scratch_shapes=[pltpu.VMEM((4, 4, 2) + s, BF) for s in FFN]
        + [pltpu.VMEM((4, 4) + s, BF) for s in shapes]
        + tokens_scratch(rows)
        + [pltpu.SemaphoreType.DMA((6 + n,)), pltpu.SemaphoreType.DMA((6 + n,))],
        compiler_params=pltpu.CompilerParams(
            collective_id=4, has_side_effects=True, vmem_limit_bytes=48 * 1024 * 1024
        ),
        name="scatter_tokens",
    )(t, hidden, cot, mid, gg, gu, wd)


def scatter_kernel(a, o, p0, p1, p2, p3, t, *refs):
    n = len(PIECES)

    def take(count):
        nonlocal refs
        head, refs = refs[:count], refs[count:]
        return head

    outs, (t_out,) = take(2 + n), take(1)
    own, got1, far2, near2, sum2 = (take(2) for _ in range(5))
    line = sum2 + take(n)
    far3, near3, fins, gots = take(2 + n), take(2 + n), take(2 + n), take(2)
    acc, far, near, send, recv, loc = refs
    ins = (a, o)
    ways = (0, 1) + tuple(p[1] for p in PIECES)
    z, x, k, c = place()
    zs = [device(plus(z, i), x, k, c) for i in (1, 3)]
    xs = [device(z, plus(x, i), k, c) for i in (1, 3)]
    ys = [device(z, x, k, plus(c, i)) for i in (1, 2, 3)]
    sibling = device(z, x, 1 - k, c)

    def spot(m, i):
        return plus(z if ways[m] else x, i)

    def piece(ref, m, p, *rest):
        return ref.at[(p, slice(None)) + rest] if ways[m] else ref.at[(slice(None), p) + rest]

    local = {}
    for i in (2, 1, 3, 0):
        for m in range(2):
            p = spot(m, i)
            copy = pltpu.make_async_copy(
                piece(ins[m], m, p, k), piece(own[m], m, p), loc.at[m * 4 + i]
            )
            copy.start()
            local[m, i] = copy
    loads = []
    for m, src in enumerate((p0, p1, p2, p3)):
        loads.append(pltpu.make_async_copy(src, line[2 + m], loc.at[8 + m]))
        loads[m].start()
    greet(zs + xs + ys + [sibling])
    cp = Copies(send, recv)
    first, second, third, closing = {}, [], {}, {}
    for i in (2, 1, 3, 0):
        for m in range(2):
            p = spot(m, i)
            first[m, i] = cp.go(piece(ins[m], m, p, 1 - k), piece(got1[m], m, p), sibling)

    def rows_of(some):
        return pl.ds(0, some.size)

    def start_third(m):
        ref, rows = line[m], halves(line[m].shape[1])

        def send(p, h):
            return ref.at[p, rows[h]]

        def add(p, h, got):
            ref[p, rows[h]] = (ref[p, rows[h]].astype(F32) + got[...].astype(F32)).astype(BF)
            return send(p, h)

        third[m] = RingScatter(
            cp,
            send,
            add,
            x if ways[m] else z,
            *(xs if ways[m] else zs),
            (far3[m].at[0, rows_of(rows[0])], far3[m].at[1, rows_of(rows[1])]),
            (lambda h: near3[m].at[0, rows[h]], lambda h: near3[m].at[1, rows[h]]),
        )
        third[m].plain()

    def close(m):
        third[m].finish()
        total = line[m][x if ways[m] else z].astype(F32)
        total = total + near3[m][0].astype(F32) + near3[m][1].astype(F32)
        if m == 2:
            outs[m][...] = total
            return
        fins[m][...] = total.reshape(fins[m].shape)
        for i in (1, 2, 3):
            target = gots[m].at[i - 1] if m < 2 else outs[m].at[c]
            closing[m, i] = cp.go(fins[m].at[plus(c, i)], target, ys[i - 1])
        if m > 2:
            outs[m][c] = fins[m][c]

    def join(m, i):
        p = spot(m, i)
        local[m, i].wait()
        first[m, i].wait_recv()

        def add(j, carry):
            at = (p, j) if ways[m] else (j, p)
            own[m][at] = (own[m][at].astype(F32) + got1[m][at].astype(F32)).astype(BF)
            return carry

        lax.fori_loop(0, 4, add, 0)

    for m in range(2):
        join(m, 2)
        second.append(
            RingScatter(
                cp,
                functools.partial(half_of, own[m], ways[m]),
                functools.partial(add_half, own[m], ways[m]),
                spot(m, 0),
                *(zs if ways[m] else xs),
                (far2[m].at[0], far2[m].at[1]),
                (
                    lambda h, m=m: near2[m].at[0, pl.ds(2 * h, 2)],
                    lambda h, m=m: near2[m].at[1, pl.ds(2 * h, 2)],
                ),
            )
        )
    for m in range(2):
        join(m, 1)
        join(m, 3)
        second[m].plain()
    for m in range(n):
        loads[m].wait()
        start_third(2 + m)
    tokens = tokens_ring(cp, t, acc, far, near, c, (ys[0], ys[2]))
    tokens.plain()
    for m in range(2):
        second[m].forward()
    for m in range(2):
        join(m, 0)
    for m in range(n):
        third[2 + m].forward()
    tokens.forward()
    for m in range(2):
        second[m].finish()
        sum_line(own[m], near2[m], line[m], ways[m], spot(m, 0))
        start_third(m)
    for m in range(n):
        close(2 + m)
    for m in range(2):
        third[m].forward()
    tokens.finish()
    t_out[...] = t[c].astype(F32) + near[0].astype(F32) + near[1].astype(F32)
    for m in range(2):
        close(m)
    for copy in closing.values():
        copy.wait_recv()
    for m in range(2):
        total = fins[m][c]
        for i in range(3):
            total = total + gots[m][i]
        outs[m][...] = total
    cp.finish()


def scatter(a, o, sums, t):
    n = len(PIECES)
    pair = [a.shape[3:], o.shape[3:]]
    shapes = pair + [s.shape[1:] for s in sums]
    quarter = [(s[0] // 4, s[1]) for s in shapes]
    outs = quarter[:2] + [shapes[2]] + [(4,) + q for q in quarter[3:]]
    scratch = []
    for lead in ((4, 4), (4, 4), (2, 2), (2, 4)):
        scratch += [pltpu.VMEM(lead + s, BF) for s in pair]
    scratch += [pltpu.VMEM((4,) + s, BF) for s in shapes]
    scratch += [pltpu.VMEM((2, halves(s[0])[1].size, s[1]), BF) for s in shapes]
    scratch += [pltpu.VMEM((2,) + s, BF) for s in shapes]
    scratch += [pltpu.VMEM((4,) + q if m != 2 else (8, 128), F32) for m, q in enumerate(quarter)]
    scratch += [pltpu.VMEM((3,) + q, F32) for q in quarter[:2]]
    scratch += tokens_scratch(t.shape[1:])
    count = 2 * 19 + 6 * n + 3 * (n - 1) + 6
    scratch += [
        pltpu.SemaphoreType.DMA((count,)),
        pltpu.SemaphoreType.DMA((count,)),
        pltpu.SemaphoreType.DMA((8 + n,)),
    ]
    return pl.pallas_call(
        scatter_kernel,
        out_shape=[jax.ShapeDtypeStruct(s, F32) for s in outs]
        + [jax.ShapeDtypeStruct(t.shape[1:], F32)],
        in_specs=[ANY] * (2 + n) + [VMEM],
        out_specs=[VMEM] * (3 + n),
        scratch_shapes=scratch,
        compiler_params=pltpu.CompilerParams(
            collective_id=5, has_side_effects=True, vmem_limit_bytes=40 * 1024 * 1024
        ),
        name="scatter_grads",
    )(a, o, *sums, t)


def rotary_tables(positions, head_size):
    half = head_size // 2
    frequency = ROTARY_BASE ** (-(jnp.arange(half, dtype=F32) * 2.0 / head_size))
    angles = positions.astype(F32)[:, None] * frequency[None, :]
    return (jnp.cos(angles), jnp.sin(angles))


def rotate(values, cosine, sine, heads, head_size):
    count = values.shape[0]
    shaped = values.reshape(count, heads, head_size)
    half = head_size // 2
    first = shaped[..., :half]
    second = shaped[..., half:]
    cos_rows = cosine[:, None, :]
    sin_rows = sine[:, None, :]
    turned = jnp.concatenate(
        [first * cos_rows - second * sin_rows, second * cos_rows + first * sin_rows], axis=-1
    )
    return turned.reshape(count, heads * head_size)


def norm_forward(values):
    factor = lax.rsqrt(jnp.mean(values * values, axis=-1, keepdims=True) + EPSILON)
    return (values * factor, factor)


def norm_backward(grad_out, normed, factor, gain):
    grad_normed = grad_out * gain
    inner = jnp.mean(grad_normed * normed, axis=-1, keepdims=True)
    return (factor * (grad_normed - normed * inner), jnp.sum(grad_out * normed, axis=0))


def dot(a, b):
    return jnp.dot(a, b, preferred_element_type=F32)


def dot_t(a, b):
    return lax.dot_general(a, b, (((1,), (1,)), ((), ())), preferred_element_type=F32)


def t_dot(a, b):
    return lax.dot_general(a, b, (((0,), (0,)), ((), ())), preferred_element_type=F32)


def choose(flags):
    return flags.astype(BF)


def local(
    block_input,
    positions,
    first_gain,
    query_weight,
    query_bias,
    key_weight,
    value_weight,
    value_bias,
    output_weight,
    second_gain,
    gate_weight,
    up_weight,
    down_weight,
    cotangent,
):
    f = lax.axis_index("fsdp")
    c = lax.axis_index("ctx")
    stretch = f * 4 + c

    i896 = jnp.arange(D)
    spread = choose((i896 + i896 // 7)[:, None] == jnp.arange(DP)[None, :])

    all_a, all_o, all_d, all_g, all_u, cot_all = gather(
        query_weight,
        key_weight,
        value_weight,
        output_weight,
        down_weight,
        gate_weight,
        up_weight,
        jnp.concatenate([query_bias, value_bias, first_gain, second_gain])[None],
        cotangent,
    )
    rows_o = all_o.reshape(32, 32, D)
    gain_first = jnp.sum(rows_o[:, 7].astype(F32), axis=0)
    gain_second = jnp.sum(rows_o[:, 15].astype(F32), axis=0)
    all_a = all_a.reshape(DP, 1152)
    cot_all = cot_all.reshape(4 * TOK, D)
    weight_output = all_o.reshape(DP, D)
    pad_ones = (jnp.arange(DP) % 8 == 7).astype(F32)[None, :]

    residual_in = block_input.astype(F32)
    normed_one, scale_one = norm_forward(residual_in)
    normed_input = (normed_one * gain_first).astype(BF)
    input_pad = (dot(normed_input, spread) + pad_ones).astype(BF)
    qkv = dot(input_pad, all_a)
    cosine, sine = rotary_tables(positions, HEAD_SIZE)
    query_rot = rotate(qkv[:, :896], cosine, sine, HEADS, HEAD_SIZE).astype(BF)
    key_rot = rotate(qkv[:, 896:1024], cosine, sine, KV_HEADS, HEAD_SIZE).astype(BF)
    value_rows = qkv[:, 1024:].astype(BF)
    first = (REACH * TOK + jnp.arange(TOK, dtype=jnp.int32) - positions)[:, None]
    seen, attended, logs, all_d, all_g, all_u = window(
        query_rot, jnp.concatenate([key_rot, value_rows], axis=1), first, (all_d, all_g, all_u)
    )
    attended_pad = dot(attended, spread).astype(BF)
    residual_mid = residual_in + dot(attended_pad, weight_output)

    normed_two, scale_two = norm_forward(residual_mid)
    normed_mid = (normed_two * gain_second).astype(BF)
    mid_all, all_d, all_g, all_u = tokens_gather(normed_mid, (all_d, all_g, all_u))
    mid_all = mid_all.reshape(4 * TOK, D)
    all_g = all_g.reshape(DP, UC)
    all_u = all_u.reshape(DP, UC)
    all_d = all_d.reshape(UC, D)
    mid_pad = dot(mid_all, spread).astype(BF)
    gate_pre = dot(mid_pad, all_g)
    up_pre = dot(mid_pad, all_u)
    sigma = jax.nn.sigmoid(gate_pre)
    hidden = (gate_pre * sigma * up_pre).astype(BF)
    grad_hidden = dot_t(cot_all, all_d)
    grad_gate_pre = (grad_hidden * up_pre * sigma * (1.0 + gate_pre * (1.0 - sigma))).astype(BF)
    grad_up_pre = (grad_hidden * gate_pre * sigma).astype(BF)
    mid_part = (dot_t(grad_gate_pre, all_g) + dot_t(grad_up_pre, all_u)).astype(BF)
    mid_part = dot_t(mid_part, spread).astype(BF)
    grad_normed_mid, out_part, *sums = tokens_sum(
        mid_part.reshape(4, TOK, D), hidden, cot_all, mid_pad, grad_gate_pre, grad_up_pre, all_d
    )
    grad_norm_part, grad_gain_two = norm_backward(
        grad_normed_mid, normed_two, scale_two, gain_second
    )
    grad_mid = cotangent.astype(F32) + grad_norm_part

    grad_mid_low = grad_mid.astype(BF)
    grad_output_w = t_dot(attended_pad, grad_mid_low)
    grad_attended = dot_t(dot_t(grad_mid_low, weight_output).astype(BF), spread).astype(BF)
    turn = jnp.stack(
        [jnp.tile(cosine, (1, 4)), jnp.tile(jnp.concatenate([sine, -sine], axis=1), (1, 2))]
    )
    lows, *sums = back(query_rot, grad_attended, attended, logs, seen, first, turn, sums)
    grad_qkv_w = t_dot(input_pad, lows)
    grad_normed_input = dot_t(dot_t(lows, all_a).astype(BF), spread)
    grad_in_part, grad_gain_one = norm_backward(
        grad_normed_input, normed_one, scale_one, gain_first
    )
    grad_input = (grad_mid + grad_in_part).astype(BF)

    group = jnp.arange(DP)[:, None] // 8
    gains = jnp.where(
        i896[None, :] // 7 == group, grad_gain_one[None, :], jnp.roll(grad_gain_two, 448)[None, :]
    )
    grad_output_w = jnp.where(jnp.arange(DP)[:, None] % 8 == 7, gains, grad_output_w)
    sum_a, sum_o, sum_d, sum_u0, sum_g, sum_u1, out_sum = scatter(
        grad_qkv_w.astype(BF).reshape(4, 4, 2, 32, 1152),
        grad_output_w.astype(BF).reshape(4, 4, 2, 32, D),
        sums,
        out_part,
    )
    sum_u = jnp.concatenate([sum_u0, sum_u1], axis=2)
    block_output = (residual_mid + out_sum).astype(BF)

    def columns(parts):
        parts = parts[:, :7].reshape(4, 7, 32, UP)[..., :UN]
        return jnp.transpose(parts, (1, 2, 0, 3)).reshape(7, FF)

    at = 7 * stretch
    return (
        block_output,
        grad_input,
        lax.dynamic_slice(sum_o[7], (at,), (7,)),
        sum_a[:7, :896],
        lax.dynamic_slice(sum_a[7], (at,), (7,)),
        sum_a[:7, 896:1024],
        sum_a[:7, 1024:1152],
        lax.dynamic_slice(sum_a[7], (1024 + stretch,), (1,)),
        sum_o[:7],
        lax.dynamic_slice(sum_o[7], (lax.rem(at + 448, 896),), (7,)),
        columns(sum_g),
        columns(sum_u),
        sum_d[:UN],
    )


def solution(mesh):
    tokens = P(("fsdp", "ctx"), None)
    entries = P(("fsdp", "ctx"))
    rows = P("fsdp", None)
    vector = P("fsdp")
    in_specs = (
        tokens,
        entries,
        vector,
        rows,
        vector,
        rows,
        rows,
        vector,
        rows,
        vector,
        rows,
        rows,
        rows,
        tokens,
    )
    out_specs = (
        tokens,
        tokens,
        entries,
        tokens,
        entries,
        tokens,
        tokens,
        entries,
        tokens,
        entries,
        tokens,
        tokens,
        tokens,
    )
    return jax.shard_map(local, mesh=mesh, in_specs=in_specs, out_specs=out_specs, check_vma=False)
```

profile of v0, /device:TPU:0, one launch (start us, length us, event | category | flops | bytes accessed | tf_op | source)
XLA Modules:
  0.0 247.0 jit_solution(17401033506383731757)
XLA Ops:
  0.6 0.8 maximum_bitcast_fusion.vec
  1.4 0.9 copy-done.16
  2.4 1.0 copy-done.28
  3.3 1.0 copy-done.29
  4.3 1.0 copy-done.32
  5.3 0.8 copy-done.40
  6.1 0.8 copy-done.41
  8.3 31.3 %gather_weights.1 = (bf16[4,4,2,32,1152]{4,3,2,1,0:T(8,128)(2,1)S(1)}, bf16[4,4,2,32,896]{4,3,2,1,0:T(8,128)(2,1)S(1)}, bf16[4,4,2,48,896]{4,3,2,1,0:T(8,128)(2,...) custom-call(bf16[28,896]{1,0:T(8,128)(2,1)S(1)} %copy-done.40, ...), custom_call_target="tpu_custom_call" | custom-call | tf_op jit(solution)/shard_map/gather_weights/pallas_call | solution.py:315
  39.6 1.8 copy-done.1
  41.7 1.3 fusion.29
  43.1 2.0 fusion.15
  45.8 0.8 copy-done.48
  46.7 0.8 fusion.38
  47.6 0.8 slice.121
  48.5 1.1 slice.94
  49.5 1.0 copy.48
  50.5 1.1 subtract_convert_fusion
  51.9 35.9 %attention_forward.1 = (bf16[9,128,256]{2,1,0:T(8,128)(2,1)S(1)}, bf16[128,896]{1,0:T(8,128)(2,1)S(1)}, f32[128,128]{1,0:T(8,128)S(1)}, bf16[4,4,2,48,896]{4,3,2...) custom-call(bf16[128,896]{1,0:T(8,128)(2,1)S(1)} %copy.51.q, ...), custom_call_target="tpu_custom_call", output_to_operand_aliasing={{3}: (3, {}), {4}: (4, {}), {5}: (5, {})} | custom-call | tf_op jit(solution)/shard_map/attention_forward/pallas_call | solution.py:413
  87.9 0.9 fusion.16
  90.2 0.8 multiply_convert_fusion.3.t
  91.0 12.6 %gather_tokens.1 = (bf16[4,128,896]{2,1,0:T(8,128)(2,1)}, bf16[4,4,2,48,896]{4,3,2,1,0:T(8,128)(2,1)}, bf16[4,4,2,32,1536]{4,3,2,1,0:T(8,128)(2,1)}, bf16[4,4,2,32,1536]{4,3,2,1,0:T(8,128)(2,1)}) custom-call(bf16[128,896]{1,0:T(8,128)(2,1)} %multiply_convert_fusion.3.t, ...), custom_call_target="tpu_custom_call", output_to_operand_aliasing={{1}: (1, {}), {2}: (2, {}), {3}: (3, {})} | custom-call | tf_op jit(solution)/shard_map/gather_tokens/pallas_call | solution.py:606
  103.6 4.0 %fusion.55 = f32[512,1536]{1,0:T(8,128)S(1)} fusion(bf16[512,896]{1,0:T(8,128)(2,1)} %bitcast.71, bf16[1536,896]{1,0:T(8,128)(2,1)} %bitcast.60), kind=kOutput, calls=%fused_computation.111 | convolution fusion | flops 1409286144 | bytes 6815744 | tf_op jit(solution)/shard_map/dot_general | solution.py:952
  107.6 1.4 fusion.12.mid
  109.5 1.8 fusion.56
  111.4 4.2 %multiply_convert_fusion = (bf16[512,1536]{1,0:T(8,128)(2,1)}, bf16[512,1536]{1,0:T(8,128)(2,1)S(1)}, bf16[512,1536]{1,0:T(8,128)(2,1)}) fusion(f32[512,1536]{1,0:T(8,128)S(1)} %fusion.56, f32[512,1536]{1,0:T(8,128)S(1)} %fusion.55, bf16[512,1024]{1,0:T(8,128)(2,1)S(1)} %fusion.12.mid, bf16[1024,1536]{1,0:T(8,128)(2,1)S(1)} %bitcast.77), kind=kOutput, calls=%fused_computation.9 | convolution fusion | flops 1623195648 | bytes 15204352 | tf_op jit(solution)/shard_map/dot_general | solution.py:948
  115.6 3.2 %fusion.57 = f32[512,1024]{1,0:T(8,128)} fusion(bf16[512,1536]{1,0:T(8,128)(2,1)S(1)} %get-tuple-element.88.gg, bf16[1024,1536]{1,0:T(8,128)(2,1)S(1)} %bitcast.63), kind=kOutput, calls=%fused_computation.113 | convolution fusion | flops 1610612736 | bytes 6815744 | tf_op jit(solution)/shard_map/dot_general | solution.py:952
  118.8 6.5 %fusion.13 = bf16[512,896]{1,0:T(8,128)(2,1)} fusion(s32[896]{0:T(1024)S(1)} %iota_add_fusion, f32[512,1024]{1,0:T(8,128)} %fusion.57, bf16[512,1536]{1,0:T(8,128)(2,1)S(1)} %copy-done.54, bf16[1024,1536]{1,0:T(8,128)(2,1)} %bitcast.76), kind=kOutput, calls=%fused_computation.21 | convolution fusion | flops 2552561664 | bytes 7736832 | tf_op jit(solution)/shard_map/dot_general | solution.py:952
  125.3 1.2 copy-done.10
  126.5 1.2 copy-done.13
  127.7 21.8 %scatter_tokens.1 = (f32[128,896]{1,0:T(8,128)S(1)}, bf16[4,128,896]{2,1,0:T(8,128)(2,1)S(1)}, bf16[4,4,48,896]{3,2,1,0:T(8,128)(2,1)}, bf16[4,4,32,768]{3,2,1,0...) custom-call(bf16[4,128,896]{2,1,0:T(8,128)(2,1)S(1)} %bitcast.73, ...), custom_call_target="tpu_custom_call" | custom-call | tf_op jit(solution)/shard_map/scatter_tokens/pallas_call | solution.py:711
  149.5 0.9 copy-done.14
  150.5 0.9 copy-done.18
  151.3 0.9 copy-done.20
  153.4 2.0 fusion.17.grad
  156.9 1.0 pad_maximum_fusion.2.turn
  157.9 1.3 copy-done.8
  159.3 1.1 copy-done.21
  160.4 1.1 copy-done.23
  161.5 0.9 copy-done.34
  162.4 0.9 copy-done.35
  163.4 30.6 %attention_backward.1 = (bf16[128,1152]{1,0:T(8,128)(2,1)S(1)}, bf16[4,48,896]{2,1,0:T(8,128)(2,1)S(1)}, bf16[4,32,768]{2,1,0:T(8,128)(2,1)S(1)}, bf16[4,32,1536...) custom-call(bf16[128,896]{1,0:T(8,128)(2,1)S(1)} %copy.51.q, bf16[128,896]{1,0:T(8,128)(2,1)S(1)} %copy-done.35, ...), custom_call_target="tpu_custom_call" | custom-call | tf_op jit(solution)/shard_map/attention_backward/pallas_call | solution.py:561
  197.6 2.7 %fusion.24 = (f32[128]{0:T(128)S(1)}, bf16[896]{0:T(1024)(128)(2,1)S(1)}, f32[128,896]{1,0:T(8,128)S(1)}) fusion(bf16[128,896]{1,0:T(8,128)(2,1)} %param.14, f32[896]{0:T(1024)S(1)} %get-tuple-element.82, f32[128]{0:T(128)S(1)} %copy-done.61, s32[896]{0:T(1024)S(1)} %iota_add_fusion, bf16[128,1152]{1,0:T(8,128)(2,1)} %copy-done.30, ...), kind=kOutput, calls=%fused_computation.37 | convolution fusion | flops 538721280 | bytes 3352320 | tf_op jit(solution)/shard_map/dot_general | solution.py:952
  200.4 1.8 select_convert_fusion
  202.3 0.8 convolution_convert_fusion
  203.1 35.5 %scatter_grads.1 = (f32[8,1152]{1,0:T(8,128)S(1)}, f32[8,896]{1,0:T(8,128)S(1)}, f32[48,896]{1,0:T(8,128)S(1)}, f32[4,8,768]{2,1,0:T(8,128)S(1)}, f32[4,8,1536]{...) custom-call(bf16[4,4,2,32,1152]{4,3,2,1,0:T(8,128)(2,1)S(1)} %bitcast.64, ...), custom_call_target="tpu_custom_call" | custom-call | tf_op jit(solution)/shard_map/scatter_grads/pallas_call | solution.py:901
  239.4 1.1 reshape.321
  241.2 1.1 reshape.319
  243.0 1.0 fusion.28
  (159 shorter events, 16.2 us)
Async XLA Ops:
  1.4 0.9 copy-start.16
  2.4 1.0 copy-start.28
  3.3 1.0 copy-start.29
  4.3 1.0 copy-start.32
  39.6 1.8 copy-start.1
  41.3 3.7 %copy-start.3 = (bf16[4,4,2,32,1152]{4,3,2,1,0:T(8,128)(2,1)}, bf16[4,4,2,32,1152]{4,3,2,1,0:T(8,128)(2,1)S(1)}, u32[]{:S(2)}) copy-start(bf16[4,4,2,32,1152]{4,3,2,1,0:T(8,128)(2,1)S(1)} %get-tuple-element.48) | copy-start | bytes 7077892
  41.4 4.3 %copy-start.5 = (bf16[4,4,2,32,896]{4,3,2,1,0:T(8,128)(2,1)}, bf16[4,4,2,32,896]{4,3,2,1,0:T(8,128)(2,1)S(1)}, u32[]{:S(2)}) copy-start(bf16[4,4,2,32,896]{4,3,2,1,0:T(8,128)(2,1)S(1)} %get-tuple-element.47) | copy-start | bytes 5505028
  41.4 4.3 %copy-start.11 = (bf16[4,128,896]{2,1,0:T(8,128)(2,1)}, bf16[4,128,896]{2,1,0:T(8,128)(2,1)S(1)}, u32[]{:S(2)}) copy-start(bf16[4,128,896]{2,1,0:T(8,128)(2,1)S(1)} %get-tuple-element.53) | copy-start | bytes 2752516
  41.4 5.3 %copy-start.63 = (s32[128]{0:T(128)S(1)}, s32[128]{0:T(128)}, u32[]{:S(2)}) copy-start(s32[128]{0:T(128)} %param.15) | copy-start | bytes 1540
  43.1 4.6 %copy-start.60 = (f32[128]{0:T(128)}, f32[128]{0:T(128)S(1)}, u32[]{:S(2)}) copy-start(f32[128]{0:T(128)S(1)} %add_rsqrt_fusion.1) | copy-start | bytes 1540
  51.9 36.9 %copy-start.6 = (bf16[4,4,2,32,896]{4,3,2,1,0:T(8,128)(2,1)S(1)}, bf16[4,4,2,32,896]{4,3,2,1,0:T(8,128)(2,1)}, u32[]{:S(2)}) copy-start(bf16[4,4,2,32,896]{4,3,2,1,0:T(8,128)(2,1)} %copy-done.5) | copy-start | bytes 5505028
  51.9 36.9 %copy-start.49 = (bf16[128,896]{1,0:T(8,128)(2,1)S(1)}, bf16[128,896]{1,0:T(8,128)(2,1)}, u32[]{:S(2)}) copy-start(bf16[128,896]{1,0:T(8,128)(2,1)} %param.14) | copy-start | bytes 688132
  87.8 1.5 copy-start.22
  87.9 3.1 %copy-start = (bf16[4,4,2,48,896]{4,3,2,1,0:T(8,128)(2,1)}, bf16[4,4,2,48,896]{4,3,2,1,0:T(8,128)(2,1)S(1)}, u32[]{:S(2)}) copy-start(bf16[4,4,2,48,896]{4,3,2,1,0:T(8,128)(2,1)S(1)} %get-tuple-element.54.d_in) | copy-start | bytes 8257540
  87.9 15.8 %copy-start.33 = (bf16[128,896]{1,0:T(8,128)(2,1)}, bf16[128,896]{1,0:T(8,128)(2,1)S(1)}, u32[]{:S(2)}) copy-start(bf16[128,896]{1,0:T(8,128)(2,1)S(1)} %get-tuple-element.52.att) | copy-start | bytes 688132
  88.8 2.1 copy-start.57
  103.6 4.0 %copy-start.62 = (bf16[4,128,896]{2,1,0:T(8,128)(2,1)S(1)}, bf16[4,128,896]{2,1,0:T(8,128)(2,1)}, u32[]{:S(2)}) copy-start(bf16[4,128,896]{2,1,0:T(8,128)(2,1)} %get-tuple-element.58) | copy-start | bytes 2752516
  107.6 1.9 copy-start.2
  109.0 2.3 copy-start.9
  109.5 1.9 copy-start.44
  115.6 3.2 %copy-start.53 = (bf16[512,1536]{1,0:T(8,128)(2,1)}, bf16[512,1536]{1,0:T(8,128)(2,1)S(1)}, u32[]{:S(2)}) copy-start(bf16[512,1536]{1,0:T(8,128)(2,1)S(1)} %get-tuple-element.88.gg) | copy-start | bytes 4718596
  115.6 3.2 %copy-start.54 = (bf16[512,1536]{1,0:T(8,128)(2,1)S(1)}, bf16[512,1536]{1,0:T(8,128)(2,1)}, u32[]{:S(2)}) copy-start(bf16[512,1536]{1,0:T(8,128)(2,1)} %get-tuple-element.89.gu) | copy-start | bytes 4718596
  118.8 6.5 %copy-start.12 = (bf16[4,128,896]{2,1,0:T(8,128)(2,1)S(1)}, bf16[4,128,896]{2,1,0:T(8,128)(2,1)}, u32[]{:S(2)}) copy-start(bf16[4,128,896]{2,1,0:T(8,128)(2,1)} %copy-done.11) | copy-start | bytes 2752516
  125.3 1.2 copy-start.10
  126.5 1.2 copy-start.13
  127.7 24.5 %copy-start.46 = (f32[128,896]{1,0:T(8,128)S(1)}, f32[128,896]{1,0:T(8,128)}, u32[]{:S(2)}) copy-start(f32[128,896]{1,0:T(8,128)} %copy-done.45) | copy-start | bytes 1376260
  127.7 25.5 %copy-start.17 = (bf16[128,896]{1,0:T(8,128)(2,1)S(1)}, bf16[128,896]{1,0:T(8,128)(2,1)}, u32[]{:S(2)}) copy-start(bf16[128,896]{1,0:T(8,128)(2,1)} %t.1) | copy-start | bytes 688132
  127.7 25.7 %copy-start.7 = (bf16[4,4,2,32,896]{4,3,2,1,0:T(8,128)(2,1)S(1)}, bf16[4,4,2,32,896]{4,3,2,1,0:T(8,128)(2,1)}, u32[]{:S(2)}) copy-start(bf16[4,4,2,32,896]{4,3,2,1,0:T(8,128)(2,1)} %copy-done.5) | copy-start | bytes 5505028
  152.2 3.2 %copy-start.58 = (f32[128,32]{0,1:T(8,128)S(1)}, f32[128,32]{0,1:T(8,128)}, u32[]{:S(2)}) copy-start(f32[128,32]{0,1:T(8,128)} %get-tuple-element.100) | copy-start | bytes 49156
  152.4 5.5 %copy-start.19 = (bf16[4,4,32,768]{3,2,1,0:T(8,128)(2,1)S(1)}, bf16[4,4,32,768]{3,2,1,0:T(8,128)(2,1)}, u32[]{:S(2)}) copy-start(bf16[4,4,32,768]{3,2,1,0:T(8,128)(2,1)} %copy-done.18) | copy-start | bytes 2359300
  153.4 2.8 %copy-start.51 = (f32[128,896]{1,0:T(8,128)}, f32[128,896]{1,0:T(8,128)S(1)}, u32[]{:S(2)}) copy-start(f32[128,896]{1,0:T(8,128)S(1)} %multiply_add_fusion) | copy-start | bytes 1376260
  156.9 40.7 %copy-start.4 = (bf16[4,4,2,32,1152]{4,3,2,1,0:T(8,128)(2,1)S(1)}, bf16[4,4,2,32,1152]{4,3,2,1,0:T(8,128)(2,1)}, u32[]{:S(2)}) copy-start(bf16[4,4,2,32,1152]{4,3,2,1,0:T(8,128)(2,1)} %copy-done.3) | copy-start | bytes 7077892
  157.9 1.3 copy-start.8
  159.3 1.1 copy-start.21
  160.4 1.1 copy-start.23
  161.5 0.9 copy-start.34
  163.4 34.2 %copy-start.61 = (f32[128]{0:T(128)S(1)}, f32[128]{0:T(128)}, u32[]{:S(2)}) copy-start(f32[128]{0:T(128)} %copy-done.60) | copy-start | bytes 1540
  197.6 2.7 %copy-start.52 = (f32[128,896]{1,0:T(8,128)S(1)}, f32[128,896]{1,0:T(8,128)}, u32[]{:S(2)}) copy-start(f32[128,896]{1,0:T(8,128)} %copy-done.51) | copy-start | bytes 1376260
  197.6 2.8 %copy-start.59 = (bf16[896]{0:T(1024)(128)(2,1)S(1)}, bf16[896]{0:T(1024)(128)(2,1)}, u32[]{:S(2)}) copy-start(bf16[896]{0:T(1024)(128)(2,1)} %pad_maximum_fusion.6) | copy-start | bytes 5380
  200.3 2.0 copy-start.31
  200.3 2.0 copy-start.56
  200.4 2.7 %copy-start.15 = (bf16[4,128,896]{2,1,0:T(8,128)(2,1)S(1)}, bf16[4,128,896]{2,1,0:T(8,128)(2,1)}, u32[]{:S(2)}) copy-start(bf16[4,128,896]{2,1,0:T(8,128)(2,1)} %copy-done.14) | copy-start | bytes 2752516
  200.4 2.7 %copy-start.25 = (bf16[4,32,1536]{2,1,0:T(8,128)(2,1)S(1)}, bf16[4,32,1536]{2,1,0:T(8,128)(2,1)}, u32[]{:S(2)}) copy-start(bf16[4,32,1536]{2,1,0:T(8,128)(2,1)} %copy-done.24) | copy-start | bytes 1179652
  200.4 2.7 %copy-start.27 = (bf16[4,48,896]{2,1,0:T(8,128)(2,1)S(1)}, bf16[4,48,896]{2,1,0:T(8,128)(2,1)}, u32[]{:S(2)}) copy-start(bf16[4,48,896]{2,1,0:T(8,128)(2,1)} %copy-done.26) | copy-start | bytes 1032196
  200.4 2.7 %copy-start.37 = (bf16[4,32,768]{2,1,0:T(8,128)(2,1)S(1)}, bf16[4,32,768]{2,1,0:T(8,128)(2,1)}, u32[]{:S(2)}) copy-start(bf16[4,32,768]{2,1,0:T(8,128)(2,1)} %copy-done.36) | copy-start | bytes 589828
  200.4 2.7 %copy-start.39 = (bf16[4,32,768]{2,1,0:T(8,128)(2,1)S(1)}, bf16[4,32,768]{2,1,0:T(8,128)(2,1)}, u32[]{:S(2)}) copy-start(bf16[4,32,768]{2,1,0:T(8,128)(2,1)} %copy-done.38) | copy-start | bytes 589828
  239.0 3.9 %copy-start.47 = (f32[128,896]{1,0:T(8,128)S(1)}, f32[128,896]{1,0:T(8,128)}, u32[]{:S(2)}) copy-start(f32[128,896]{1,0:T(8,128)} %copy-done.45) | copy-start | bytes 1376260
  239.0 3.9 %copy-start.50 = (bf16[128,896]{1,0:T(8,128)(2,1)S(1)}, bf16[128,896]{1,0:T(8,128)(2,1)}, u32[]{:S(2)}) copy-start(bf16[128,896]{1,0:T(8,128)(2,1)} %param.14) | copy-start | bytes 688132
  (16 other events, 12.5 us)
where the time goes:
time: 248 us; the launch traced here: 247 us
  Pallas kernels  168 us (68%)
  local copies, waits for them, and re-layouts  37.2 us (15%)
  matrix products  32.4 us (13%)
  other arithmetic  8.31 us (3%)
    pallas_call x1, Pallas kernels, window(): pl.pallas_call(window_kernel, out_shape=[jax.ShapeDtypeStruct((REACH + 1,...  35.9 us
    pallas_call x1, Pallas kernels, scatter(): pl.pallas_call(scatter_kernel, out_shape=[jax.ShapeDtypeStruct(s, F32) fo...  35.5 us
    pallas_call x1, Pallas kernels, gather(): pl.pallas_call(gather_kernel, out_shape=[out(*p) for p in packed] + [jax....  31.3 us
    pallas_call x1, Pallas kernels, back(): pl.pallas_call(back_kernel, out_shape=[jax.ShapeDtypeStruct((TOK, 1152),...  30.6 us
    unnamed x129, local copies, waits for them, and re-layouts  25.7 us
    pallas_call x1, Pallas kernels, tokens_sum(): pl.pallas_call(tokens_sum_kernel, out_shape=[jax.ShapeDtypeStruct(rows, F...  21.8 us
    dot_general x5, matrix products, dot_t(): lax.dot_general(a, b, (((1,), (1,)), ((), ())), preferred_element_type=F32)  18.3 us
    pallas_call x1, Pallas kernels, tokens_gather(): pl.pallas_call(tokens_kernel, out_shape=[jax.ShapeDtypeStruct((4,) + t.sh...  12.6 us

commit v1 on v0

--- a/solution.py
+++ b/solution.py
@@ -29,6 +29,8 @@
 F32 = jnp.float32
 ANY = pl.BlockSpec(memory_space=pl.ANY)
 VMEM = pl.BlockSpec(memory_space=pltpu.VMEM)
+HBM = pl.BlockSpec(memory_space=pltpu.HBM)
+VMEM_FORWARD = 58 * 1024 * 1024
 
 
 def place():
@@ -166,16 +168,79 @@
     return rings
 
 
-def gather_kernel(q, kw, v, o, down, gate, up, vec, t, *refs):
-    ao, oo, do, go, uo, to = refs[:6]
-    wq, wk, wv, wo, wd, wg, wu, units, own_a, own_o, own_d, own_g, own_u = refs[6:19]
-    send, recv, load, loc = refs[19:]
+def stretch_device(i):
+    i = lax.rem(i + 128, 128)
+    return (i // 4, lax.rem(i, 4))
+
+
+def iota(shape, axis):
+    return lax.broadcasted_iota(jnp.int32, shape, axis)
+
+
+def head_move(head, scale):
+    i, j = iota((128, 128), 0), iota((128, 128), 1)
+    half, group = head % 2, head // (HEADS // KV_HEADS)
+    hit = (i // 64 == half) & (j // 64 == group) & (i % 64 == j % 64)
+    return (hit.astype(F32) * scale).astype(BF)
+
+
+def spread_heads(src, out, scale):
+    for pair in range(HEADS // 2):
+        tile = src[:, pair * 128 : (pair + 1) * 128]
+        for head in (2 * pair, 2 * pair + 1):
+            out[head] = dot(tile, head_move(head, scale)).astype(BF)
+
+
+def join_heads(src, out):
+    for pair in range(HEADS // 2):
+        total = 0.0
+        for head in (2 * pair, 2 * pair + 1):
+            total = total + dot_t(src[head], head_move(head, 1.0))
+        out[:, pair * 128 : (pair + 1) * 128] = total.astype(BF)
+
+
+def seen_mask(first_key):
+    key = iota((TOK, (REACH + 1) * TOK), 1)
+    query = REACH * TOK + iota((TOK, 1), 0)
+    return (key >= first_key) & (key <= query)
+
+
+def where(flags):
+    return flags.astype(F32).astype(BF)
+
+
+def spread_matrix():
+    i, j = iota((D, DP), 0), iota((D, DP), 1)
+    return where(i + i // 7 == j)
+
+
+def rotary(pos, freq):
+    angles = pos[...].astype(F32) * freq[...]
+    sign = jnp.where(iota((TOK, 128), 1) % 64 < 32, 1.0, -1.0)
+    return jnp.cos(angles), jnp.sin(angles) * sign
+
+
+def turned(values, cosine, sine):
+    low = iota(values.shape, 1) % 64 < 32
+    other = jnp.where(low, pltpu.roll(values, 96, 1), pltpu.roll(values, 32, 1))
+    return values * cosine + other * sine
+
+
+def forward_kernel(q, kw, v, o, down, gate, up, vec, t, block, pos, freq, *refs):
+    ao, oo, do, go, uo, to, mo, seen, qo, att, logs, mid, gains, turn = refs[:14]
+    wq, wk, wv, wo, wd, wg, wu, units, own_a, own_o, own_d, own_g, own_u = refs[14:27]
+    spread, kv, low, qs, os, send, recv, load, loc = refs[27:]
     z, x, k, c = place()
     f = lax.axis_index("fsdp")
+    me = f * 4 + c
     zs = [device(plus(z, i), x, k, c) for i in (1, 3)]
     xs = [device(z, plus(x, i), k, c) for i in (1, 3)]
     ys = [device(z, x, k, plus(c, i)) for i in (1, 3)]
     sibling = device(z, x, 1 - k, c)
+    barrier = pltpu.get_barrier_semaphore()
+    window = [stretch_device(me - o) for o in range(1, REACH + 1)]
+    for device_id in zs + xs + ys + [sibling] + window:
+        pl.semaphore_signal(barrier, inc=1, device_id=device_id, device_id_type=MESH)
     loads = [
         pltpu.make_async_copy(src, dst, load.at[i])
         for i, (src, dst) in enumerate(
@@ -186,38 +251,27 @@
         copy.start()
     token_copy = pltpu.make_async_copy(t, to.at[c], loc.at[5])
     token_copy.start()
-    for n, device_id in enumerate(zs + xs + ys + [sibling]):
-        pl.semaphore_signal(
-            pltpu.get_barrier_semaphore(), inc=1, device_id=device_id, device_id_type=MESH
-        )
-
-    def iota(shape, axis):
-        return lax.broadcasted_iota(jnp.int32, shape, axis)
-
-    def where(flags):
-        return flags.astype(F32).astype(BF)
 
     i = iota((32, 28), 1)
-    spread = where(i + i // 7 == iota((32, 28), 0))
+    rows28 = where(i + i // 7 == iota((32, 28), 0))
     row = iota((32, 1), 0)
     i, j = iota((88, 1152), 0), iota((88, 1152), 1)
     place_at = jnp.where(i < 28, 28 * f + i, jnp.where(i < 32, 1024 + 4 * f + i - 28, -1))
-    extra = dot(vec[...], where(place_at == j))
-    extra = jnp.where(row == 7, extra, 0.0)
+    extra = jnp.where(row == 7, dot(vec[...], where(place_at == j)), 0.0)
     for copy in loads[:3]:
         copy.wait()
-    own_a[:, :896] = (dot(spread, wq[...]) + extra[:, :896]).astype(BF)
-    own_a[:, 896:1024] = dot(spread, wk[...]).astype(BF)
-    own_a[:, 1024:] = (dot(spread, wv[...]) + extra[:, 1024:]).astype(BF)
+    own_a[:, :896] = (dot(rows28, wq[...]) + extra[:, :896]).astype(BF)
+    own_a[:, 896:1024] = dot(rows28, wk[...]).astype(BF)
+    own_a[:, 1024:] = (dot(rows28, wv[...]) + extra[:, 1024:]).astype(BF)
     i, j = iota((88, D), 0), iota((88, D), 1)
     one = dot(vec[...], where((i >= 32) & (i < 60) & (28 * f + i - 32 == j)))
     two = dot(vec[...], where((i >= 60) & (28 * f + i - 60 == j)))
     loads[3].wait()
     own_o[...] = (
-        dot(spread, wo[...]) + jnp.where(row == 7, one, 0.0) + jnp.where(row == 15, two, 0.0)
+        dot(rows28, wo[...]) + jnp.where(row == 7, one, 0.0) + jnp.where(row == 15, two, 0.0)
     ).astype(BF)
 
-    pl.semaphore_wait(pltpu.get_barrier_semaphore(), 7)
+    pl.semaphore_wait(barrier, 7 + REACH)
     cp = Copies(send, recv)
     ways = (0, 1)
     own, outs = (own_a, own_o), (ao, oo)
@@ -240,7 +294,7 @@
 
         first.append(RingGather(cp, part, mine, x if ways[m] else z, *(xs if ways[m] else zs)))
         keep(own[m], outs[m])
-    rows = halves(t.shape[0])
+    rows = halves(TOK)
     tokens = RingGather(cp, lambda p, h: to.at[p, rows[h]], lambda h: t.at[rows[h]], c, *ys)
 
     loads[6].wait()
@@ -248,16 +302,10 @@
     own_d[...] = dot(where(jnp.where(i < UN, i + UN * c, -1) == j), wd[...]).astype(BF)
     j = iota((1, 16 * UP), 1)
     wanted = jnp.where(j % UP < UN, (j // UP) * 152 + j % UP, -1000) + UN * c
+    for m in range(2):
+        first[m].forward()
     for r in range(19):
         units[r * 128 : (r + 1) * 128] = where(iota((128, 16 * UP), 0) + r * 128 == wanted)
-    for m in range(2):
-        first[m].forward()
-    for copy, src, out in ((loads[4], wg, own_g), (loads[5], wu, own_u)):
-        copy.wait()
-        wide = dot(spread, src[...]).astype(BF)
-        for h in range(2):
-            some = dot(wide[:, h * 2432 : (h + 1) * 2432], units[...])
-            out[:, h * 768 : (h + 1) * 768] = some.astype(BF)
     for m in range(2):
         first[m].near()
         first[m].far()
@@ -271,9 +319,6 @@
         second.append(
             RingGather(cp, part, functools.partial(part, p), p, *(zs if ways[m] else xs))
         )
-    line = start_line(cp, (z, x, k, c, zs, xs), (do, go, uo), (own_d, own_g, own_u))
-    for src, out in ((own_d, do), (own_g, go), (own_u, uo)):
-        keep(src, out)
 
     def pass_on(m, i):
         p = plus(z if ways[m] else x, i)
@@ -282,159 +327,147 @@
 
     for m in range(2):
         pass_on(m, 0)
+    for copy, src, out in ((loads[4], wg, own_g), (loads[5], wu, own_u)):
+        copy.wait()
+        wide = dot(rows28, src[...]).astype(BF)
+        for h in range(2):
+            some = dot(wide[:, h * 2432 : (h + 1) * 2432], units[...])
+            out[:, h * 768 : (h + 1) * 768] = some.astype(BF)
     for m in range(2):
         second[m].forward()
+    spot = (z, x, k, c, zs, xs)
+    line = start_line(cp, spot, (do, go, uo), (own_d, own_g, own_u))
+    for src, out in ((own_d, do), (own_g, go), (own_u, uo)):
+        keep(src, out)
     tokens.forward()
-    for ring in line:
-        ring.forward()
+    spread[...] = spread_matrix()
+    cosine, sine = rotary(pos, freq)
+    turn[0] = cosine
+    turn[1] = sine
     for m in range(2):
         second[m].near()
         pass_on(m, 1)
         pass_on(m, 3)
+    for ring in line:
+        ring.forward()
     for m in range(2):
         second[m].far()
         pass_on(m, 2)
-    for ring in line + [tokens]:
-        ring.near()
-        ring.far()
-    token_copy.wait()
     for copy in local[2:]:
         copy.wait()
     for copy in third:
         copy.wait_recv()
+    for ring in line:
+        ring.near()
+        ring.far()
+    plane = start_plane(cp, spot, (do, go, uo))
+
+    i, j = iota((8, DP), 0), iota((8, DP), 1)
+    both = dot(where(j % 32 == 7 + 8 * i), oo[...].reshape(DP, D))
+    gains[...] = both
+    residual = block[...].astype(F32)
+    factor = lax.rsqrt(jnp.mean(residual * residual, axis=-1, keepdims=True) + EPSILON)
+    normed = (residual * factor * both[0:1]).astype(BF)
+    pad = jnp.where(iota((TOK, DP), 1) % 8 == 7, 1.0, dot(normed, spread[...])).astype(BF)
+    qkv = dot(pad, ao[...].reshape(DP, 1152))
+    kv[:, :128] = turned(qkv[:, 896:1024], cosine, -sine).astype(BF)
+    kv[:, 128:] = qkv[:, 1024:].astype(BF)
+    copies = [
+        cp.go(kv, seen.at[REACH - o], stretch_device(me + o)) for o in range(REACH, 0, -1)
+    ]
+    seen[REACH] = kv[...]
+    for pair in range(HEADS // 2):
+        some = slice(pair * 128, (pair + 1) * 128)
+        qo[:, some] = turned(qkv[:, some], cosine, -sine).astype(BF)
+    spread_heads(qo, qs, 1.0 / math.sqrt(HEAD_SIZE))
+    logs[...] = jnp.zeros(logs.shape, F32)
+    first_key = REACH * TOK + iota((TOK, 1), 0) - pos[...]
+    for copy in copies:
+        copy.wait_recv()
+    for ring in plane:
+        ring.forward()
+
+    def one_head(head, carry):
+        keys = seen[:, :, :128].reshape((REACH + 1) * TOK, 128)
+        values = seen[:, :, 128:].reshape((REACH + 1) * TOK, 128)
+        scores = jnp.where(seen_mask(first_key), dot_t(qs[head], keys), -jnp.inf)
+        top = jnp.max(scores, axis=1, keepdims=True)
+        weights = jnp.exp(scores - top)
+        total = jnp.sum(weights, axis=1, keepdims=True)
+        os[head] = dot((weights * (1.0 / total)).astype(BF), values).astype(BF)
+        logs[...] += jnp.where(iota((TOK, 128), 1) == head, top + jnp.log(total), 0.0)
+        return carry
+
+    lax.fori_loop(0, HEADS, one_head, 0)
+    join_heads(os, att)
+    att_pad = dot(att[...], spread[...]).astype(BF)
+    middle = residual + dot(att_pad, oo[...].reshape(DP, D))
+    mid[...] = middle
+    factor = lax.rsqrt(jnp.mean(middle * middle, axis=-1, keepdims=True) + EPSILON)
+    low[...] = (middle * factor * both[1:2]).astype(BF)
+    mid_ring = RingGather(cp, lambda p, h: mo.at[p, rows[h]], lambda h: low.at[rows[h]], c, *ys)
+    mo[c] = low[...]
+    for ring in plane:
+        ring.near()
+        ring.far()
+    last = [cp.go(ref.at[:, :, k], ref.at[:, :, k], sibling) for ref in (go, uo, do)]
+    tokens.near()
+    tokens.far()
+    token_copy.wait()
+    mid_ring.forward()
+    mid_ring.near()
+    mid_ring.far()
+    for copy in last:
+        copy.wait_recv()
     cp.finish()
 
 
-def gather(q, kw, v, o, down, gate, up, vec, t):
+def forward(weights, vec, t, block, pos, freq):
     def out(rows, columns):
         return jax.ShapeDtypeStruct((4, 4, 2, rows, columns), BF)
 
-    weights = (q, kw, v, o, down, gate, up)
     packed = ((32, 1152), (32, D)) + FFN
-    count = 16 * 2 + 6 + 6 * len(PIECES)
+    count = 16 * 2 + 6 + 12 * len(PIECES) + REACH + 3 + 6
+    group = jax.ShapeDtypeStruct((4,) + t.shape, BF)
+    rows = jax.ShapeDtypeStruct((TOK, D), BF)
     return pl.pallas_call(
-        gather_kernel,
-        out_shape=[out(*p) for p in packed] + [jax.ShapeDtypeStruct((4,) + t.shape, BF)],
-        in_specs=[ANY] * 7 + [VMEM, ANY],
-        out_specs=[ANY] * 6,
+        forward_kernel,
+        out_shape=[out(*p) for p in packed]
+        + [
+            group,
+            group,
+            jax.ShapeDtypeStruct((REACH + 1, TOK, 256), BF),
+            rows,
+            rows,
+            jax.ShapeDtypeStruct((TOK, 128), F32),
+            jax.ShapeDtypeStruct((TOK, D), F32),
+            jax.ShapeDtypeStruct((8, D), F32),
+            jax.ShapeDtypeStruct((2, TOK, 128), F32),
+        ],
+        in_specs=[HBM] * 7 + [VMEM] + [HBM] + [VMEM] * 3,
+        out_specs=[VMEM] * 14,
         scratch_shapes=[pltpu.VMEM(w.shape, BF) for w in weights]
         + [pltpu.VMEM((2432, 16 * UP), BF)]
         + [pltpu.VMEM(p, BF) for p in packed]
         + [
+            pltpu.VMEM((D, DP), BF),
+            pltpu.VMEM((TOK, 256), BF),
+            pltpu.VMEM((TOK, D), BF),
+            pltpu.VMEM((HEADS, TOK, 128), BF),
+            pltpu.VMEM((HEADS, TOK, 128), BF),
             pltpu.SemaphoreType.DMA((count,)),
             pltpu.SemaphoreType.DMA((count,)),
             pltpu.SemaphoreType.DMA((7,)),
             pltpu.SemaphoreType.DMA((6,)),
         ],
         compiler_params=pltpu.CompilerParams(
-            collective_id=0, has_side_effects=True, vmem_limit_bytes=40 * 1024 * 1024
+            collective_id=0, has_side_effects=True, vmem_limit_bytes=VMEM_FORWARD
         ),
-        name="gather_weights",
-    )(*weights, vec, t)
-
-
-def stretch_device(i):
-    i = lax.rem(i + 128, 128)
-    return (i // 4, lax.rem(i, 4))
-
-
-def iota(shape, axis):
-    return lax.broadcasted_iota(jnp.int32, shape, axis)
-
-
-def head_move(head, scale):
-    i, j = iota((128, 128), 0), iota((128, 128), 1)
-    half, group = head % 2, head // (HEADS // KV_HEADS)
-    hit = (i // 64 == half) & (j // 64 == group) & (i % 64 == j % 64)
-    return (hit.astype(F32) * scale).astype(BF)
-
-
-def spread_heads(src, out, scale):
-    for pair in range(HEADS // 2):
-        tile = src[:, pair * 128 : (pair + 1) * 128]
-        for head in (2 * pair, 2 * pair + 1):
-            out[head] = dot(tile, head_move(head, scale)).astype(BF)
-
-
-def join_heads(src, out):
-    for pair in range(HEADS // 2):
-        total = 0.0
-        for head in (2 * pair, 2 * pair + 1):
-            total = total + dot_t(src[head], head_move(head, 1.0))
-        out[:, pair * 128 : (pair + 1) * 128] = total.astype(BF)
-
-
-def seen_mask(first):
-    key = iota((TOK, (REACH + 1) * TOK), 1)
-    query = REACH * TOK + iota((TOK, 1), 0)
-    return (key >= first[...]) & (key <= query)
-
-
-def window_kernel(q, kv, first, d_in, g_in, u_in, out, att, logs, do, go, uo, qs, os, send, recv):
-    me = lax.axis_index("fsdp") * 4 + lax.axis_index("ctx")
-    z, x, k, c = place()
-    zs = [device(plus(z, i), x, k, c) for i in (1, 3)]
-    xs = [device(z, plus(x, i), k, c) for i in (1, 3)]
-    greet([stretch_device(me - o) for o in range(1, REACH + 1)] + zs + xs)
-    cp = Copies(send, recv)
-    copies = [
-        cp.go(kv, out.at[REACH - o], stretch_device(me + o)) for o in range(REACH, 0, -1)
-    ]
-    plane = start_plane(cp, (z, x, k, c, zs, xs), (do, go, uo))
-    out[REACH] = kv[...]
-    spread_heads(q, qs, 1.0 / math.sqrt(HEAD_SIZE))
-    logs[...] = jnp.zeros(logs.shape, F32)
-    for copy in copies:
-        copy.wait_recv()
-    for ring in plane:
-        ring.forward()
-
-    def one(head, carry):
-        keys = out[:, :, :128].reshape((REACH + 1) * TOK, 128)
-        values = out[:, :, 128:].reshape((REACH + 1) * TOK, 128)
-        scores = jnp.where(seen_mask(first), dot_t(qs[head], keys), -jnp.inf)
-        top = jnp.max(scores, axis=1, keepdims=True)
-        weights = jnp.exp(scores - top)
-        total = jnp.sum(weights, axis=1, keepdims=True)
-        os[head] = dot((weights * (1.0 / total)).astype(BF), values).astype(BF)
-        logs[...] += jnp.where(iota((TOK, 128), 1) == head, top + jnp.log(total), 0.0)
-        return carry
-
-    lax.fori_loop(0, HEADS, one, 0)
-    join_heads(os, att)
-    for ring in plane:
-        ring.near()
-        ring.far()
-    cp.finish()
-
-
-def window(q, kv, first, weights):
-    count = REACH + 6 * len(PIECES)
-    return pl.pallas_call(
-        window_kernel,
-        out_shape=[
-            jax.ShapeDtypeStruct((REACH + 1,) + kv.shape, BF),
-            jax.ShapeDtypeStruct(q.shape, BF),
-            jax.ShapeDtypeStruct((TOK, 128), F32),
-        ]
-        + [jax.ShapeDtypeStruct(w.shape, BF) for w in weights],
-        in_specs=[VMEM] * 3 + [ANY] * 3,
-        out_specs=[VMEM] * 3 + [ANY] * 3,
-        input_output_aliases={3: 3, 4: 4, 5: 5},
-        scratch_shapes=[
-            pltpu.VMEM((HEADS, TOK, 128), BF),
-            pltpu.VMEM((HEADS, TOK, 128), BF),
-            pltpu.SemaphoreType.DMA((count,)),
-            pltpu.SemaphoreType.DMA((count,)),
-        ],
-        compiler_params=pltpu.CompilerParams(
-            collective_id=1, has_side_effects=True, vmem_limit_bytes=48 * 1024 * 1024
-        ),
-        name="attention_forward",
-    )(q, kv, first, *weights)
-
-
-def back_kernel(q, grad, att, logs, seen, first, turn, *refs):
+        name="forward",
+    )(*weights, vec, t, block, pos, freq)
+
+
+def back_kernel(q, grad, att, logs, seen, pos, turn, *refs):
     n = len(PIECES)
 
     def take(count):
@@ -477,14 +510,10 @@
     spread_heads(q, qs, 1.0 / math.sqrt(HEAD_SIZE))
     spread_heads(grad, gs, 1.0)
     spread_heads(att, os, 1.0)
+    first_key = REACH * TOK + iota((TOK, 1), 0) - pos[...]
     rows = (REACH + 1) * TOK
     grad_keys[...] = jnp.zeros((rows, 128), F32)
     grad_values[...] = jnp.zeros((rows, 128), F32)
-
-    def turned(values):
-        low = iota(values.shape, 1) % 64 < 32
-        other = jnp.where(low, pltpu.roll(values, 96, 1), pltpu.roll(values, 32, 1))
-        return values * turn[0] + other * turn[1]
 
     def one(head, carry):
         keys = seen[:, :, :128].reshape(rows, 128)
@@ -494,13 +523,13 @@
         delta = jnp.sum(
             gs[head].astype(F32) * os[head].astype(F32), axis=1, keepdims=True
         )
-        scores = jnp.where(seen_mask(first), dot_t(qs[head], keys), -jnp.inf)
+        scores = jnp.where(seen_mask(first_key), dot_t(qs[head], keys), -jnp.inf)
         probability = jnp.exp(scores - log_total)
         grad_scores = (probability * (dot_t(gs[head], values) - delta)).astype(BF)
         grad_values[...] += t_dot(probability.astype(BF), gs[head])
         grad_keys[...] += t_dot(grad_scores, qs[head])
         grad_query = dot(grad_scores, keys) * (1.0 / math.sqrt(HEAD_SIZE))
-        os[head] = turned(grad_query).astype(BF)
+        os[head] = turned(grad_query, turn[0], turn[1]).astype(BF)
         return carry
 
     lax.fori_loop(0, HEADS // 2, one, 0)
@@ -523,7 +552,7 @@
     for o in range(REACH):
         total_keys = total_keys + got[o, :, :128].astype(F32)
         total_values = total_values + got[o, :, 128:].astype(F32)
-    out[:, 896:1024] = turned(total_keys).astype(BF)
+    out[:, 896:1024] = turned(total_keys, turn[0], turn[1]).astype(BF)
     out[:, 1024:] = total_values.astype(BF)
     cp.finish()
 
@@ -553,7 +582,7 @@
     lax.fori_loop(0, 4, one, 0)
 
 
-def back(q, grad, att, logs, seen, first, turn, arrays):
+def back(q, grad, att, logs, seen, pos, turn, arrays):
     n = len(PIECES)
     shapes = [s.shape[2:] for s in arrays]
     count = REACH + 6 * n
@@ -576,44 +605,10 @@
             pltpu.SemaphoreType.DMA((n,)),
         ],
         compiler_params=pltpu.CompilerParams(
-            collective_id=2, has_side_effects=True, vmem_limit_bytes=48 * 1024 * 1024
+            collective_id=2, has_side_effects=True, vmem_limit_bytes=58 * 1024 * 1024
         ),
         name="attention_backward",
-    )(q, grad, att, logs, seen, first, turn, *arrays)
-
-
-def tokens_kernel(t, d_in, g_in, u_in, out, do, go, uo, send, recv):
-    z, x, k, c = place()
-    ys = [device(z, x, k, plus(c, i)) for i in (1, 3)]
-    sibling = device(z, x, 1 - k, c)
-    greet(ys + [sibling])
-    cp = Copies(send, recv)
-    rows = halves(t.shape[0])
-    ring = RingGather(cp, lambda p, h: out.at[p, rows[h]], lambda h: t.at[rows[h]], c, *ys)
-    copies = []
-    for ref in (go, uo, do):
-        copies.append(cp.go(ref.at[:, :, k], ref.at[:, :, k], sibling))
-    out[c] = t[...]
-    ring.forward()
-    ring.near()
-    ring.far()
-    for copy in copies:
-        copy.wait_recv()
-    cp.finish()
-
-
-def tokens_gather(t, weights):
-    return pl.pallas_call(
-        tokens_kernel,
-        out_shape=[jax.ShapeDtypeStruct((4,) + t.shape, BF)]
-        + [jax.ShapeDtypeStruct(w.shape, BF) for w in weights],
-        in_specs=[VMEM] + [ANY] * 3,
-        out_specs=[VMEM] + [ANY] * 3,
-        input_output_aliases={1: 1, 2: 2, 3: 3},
-        scratch_shapes=[pltpu.SemaphoreType.DMA((9,)), pltpu.SemaphoreType.DMA((9,))],
-        compiler_params=pltpu.CompilerParams(collective_id=3, has_side_effects=True),
-        name="gather_tokens",
-    )(t, *weights)
+    )(q, grad, att, logs, seen, pos, turn, *arrays)
 
 
 def tokens_ring(cp, t, acc, far, near, c, ys):
@@ -719,7 +714,7 @@
         + tokens_scratch(rows)
         + [pltpu.SemaphoreType.DMA((6 + n,)), pltpu.SemaphoreType.DMA((6 + n,))],
         compiler_params=pltpu.CompilerParams(
-            collective_id=4, has_side_effects=True, vmem_limit_bytes=48 * 1024 * 1024
+            collective_id=4, has_side_effects=True, vmem_limit_bytes=58 * 1024 * 1024
         ),
         name="scatter_tokens",
     )(t, hidden, cot, mid, gg, gu, wd)
@@ -906,31 +901,10 @@
         out_specs=[VMEM] * (3 + n),
         scratch_shapes=scratch,
         compiler_params=pltpu.CompilerParams(
-            collective_id=5, has_side_effects=True, vmem_limit_bytes=40 * 1024 * 1024
+            collective_id=5, has_side_effects=True, vmem_limit_bytes=58 * 1024 * 1024
         ),
         name="scatter_grads",
     )(a, o, *sums, t)
-
-
-def rotary_tables(positions, head_size):
-    half = head_size // 2
-    frequency = ROTARY_BASE ** (-(jnp.arange(half, dtype=F32) * 2.0 / head_size))
-    angles = positions.astype(F32)[:, None] * frequency[None, :]
-    return (jnp.cos(angles), jnp.sin(angles))
-
-
-def rotate(values, cosine, sine, heads, head_size):
-    count = values.shape[0]
-    shaped = values.reshape(count, heads, head_size)
-    half = head_size // 2
-    first = shaped[..., :half]
-    second = shaped[..., half:]
-    cos_rows = cosine[:, None, :]
-    sin_rows = sine[:, None, :]
-    turned = jnp.concatenate(
-        [first * cos_rows - second * sin_rows, second * cos_rows + first * sin_rows], axis=-1
-    )
-    return turned.reshape(count, heads * head_size)
 
 
 def norm_forward(values):
@@ -983,48 +957,55 @@
     i896 = jnp.arange(D)
     spread = choose((i896 + i896 // 7)[:, None] == jnp.arange(DP)[None, :])
 
-    all_a, all_o, all_d, all_g, all_u, cot_all = gather(
-        query_weight,
-        key_weight,
-        value_weight,
-        output_weight,
-        down_weight,
-        gate_weight,
-        up_weight,
+    half = HEAD_SIZE // 2
+    frequency = ROTARY_BASE ** (-(jnp.arange(half, dtype=F32) * 2.0 / HEAD_SIZE))
+    places = positions[:, None]
+    (
+        all_a,
+        all_o,
+        all_d,
+        all_g,
+        all_u,
+        cot_all,
+        mid_all,
+        seen,
+        query_rot,
+        attended,
+        logs,
+        residual_mid,
+        gains,
+        turn,
+    ) = forward(
+        (
+            query_weight,
+            key_weight,
+            value_weight,
+            output_weight,
+            down_weight,
+            gate_weight,
+            up_weight,
+        ),
         jnp.concatenate([query_bias, value_bias, first_gain, second_gain])[None],
         cotangent,
+        block_input,
+        places,
+        jnp.tile(frequency, 4)[None],
     )
-    rows_o = all_o.reshape(32, 32, D)
-    gain_first = jnp.sum(rows_o[:, 7].astype(F32), axis=0)
-    gain_second = jnp.sum(rows_o[:, 15].astype(F32), axis=0)
+    gain_first, gain_second = gains[0], gains[1]
     all_a = all_a.reshape(DP, 1152)
+    weight_output = all_o.reshape(DP, D)
+    all_g = all_g.reshape(DP, UC)
+    all_u = all_u.reshape(DP, UC)
+    all_d = all_d.reshape(UC, D)
     cot_all = cot_all.reshape(4 * TOK, D)
-    weight_output = all_o.reshape(DP, D)
+    mid_all = mid_all.reshape(4 * TOK, D)
     pad_ones = (jnp.arange(DP) % 8 == 7).astype(F32)[None, :]
-
     residual_in = block_input.astype(F32)
     normed_one, scale_one = norm_forward(residual_in)
     normed_input = (normed_one * gain_first).astype(BF)
     input_pad = (dot(normed_input, spread) + pad_ones).astype(BF)
-    qkv = dot(input_pad, all_a)
-    cosine, sine = rotary_tables(positions, HEAD_SIZE)
-    query_rot = rotate(qkv[:, :896], cosine, sine, HEADS, HEAD_SIZE).astype(BF)
-    key_rot = rotate(qkv[:, 896:1024], cosine, sine, KV_HEADS, HEAD_SIZE).astype(BF)
-    value_rows = qkv[:, 1024:].astype(BF)
-    first = (REACH * TOK + jnp.arange(TOK, dtype=jnp.int32) - positions)[:, None]
-    seen, attended, logs, all_d, all_g, all_u = window(
-        query_rot, jnp.concatenate([key_rot, value_rows], axis=1), first, (all_d, all_g, all_u)
-    )
     attended_pad = dot(attended, spread).astype(BF)
-    residual_mid = residual_in + dot(attended_pad, weight_output)
-
     normed_two, scale_two = norm_forward(residual_mid)
-    normed_mid = (normed_two * gain_second).astype(BF)
-    mid_all, all_d, all_g, all_u = tokens_gather(normed_mid, (all_d, all_g, all_u))
-    mid_all = mid_all.reshape(4 * TOK, D)
-    all_g = all_g.reshape(DP, UC)
-    all_u = all_u.reshape(DP, UC)
-    all_d = all_d.reshape(UC, D)
     mid_pad = dot(mid_all, spread).astype(BF)
     gate_pre = dot(mid_pad, all_g)
     up_pre = dot(mid_pad, all_u)
@@ -1046,10 +1027,7 @@
     grad_mid_low = grad_mid.astype(BF)
     grad_output_w = t_dot(attended_pad, grad_mid_low)
     grad_attended = dot_t(dot_t(grad_mid_low, weight_output).astype(BF), spread).astype(BF)
-    turn = jnp.stack(
-        [jnp.tile(cosine, (1, 4)), jnp.tile(jnp.concatenate([sine, -sine], axis=1), (1, 2))]
-    )
-    lows, *sums = back(query_rot, grad_attended, attended, logs, seen, first, turn, sums)
+    lows, *sums = back(query_rot, grad_attended, attended, logs, seen, places, turn, sums)
     grad_qkv_w = t_dot(input_pad, lows)
     grad_normed_input = dot_t(dot_t(lows, all_a).astype(BF), spread)
     grad_in_part, grad_gain_one = norm_backward(

time: 248 us -> 234 us (0.944)
  local copies, waits for them, and re-layouts: 37.2 us -> 16.1 us
  Pallas kernels: 168 us -> 173 us
    unnamed x129 -> x27, local copies, waits for them, and re-layouts: 25.7 us -> 1.28 us
    dot_general x2, matrix products: 2.64 us -> 6 us  [t_dot(): lax.dot_general(a, b, (((0,), (0,)), ((), ())), preferred_element_type=F32)]
    dot_general x7 -> x3, matrix products: 11.4 us -> 8.49 us  [dot(): return jnp.dot(a, b, preferred_element_type=F32)]
    pallas_call x3 -> x1, Pallas kernels: 79.8 us -> 82.5 us  [forward(): pl.pallas_call(forward_kernel, out_shape=[out(*p) for p in packed] + [gro...]
where the time goes in v1:
time: 234 us; the launch traced here: 233 us
  Pallas kernels  173 us (74%)
  matrix products  32.9 us (14%)
  local copies, waits for them, and re-layouts  16.1 us (7%)
  other arithmetic  9.81 us (4%)
    pallas_call x1, Pallas kernels, forward(): pl.pallas_call(forward_kernel, out_shape=[out(*p) for p in packed] + [gro...  82.5 us
    pallas_call x1, Pallas kernels, scatter(): pl.pallas_call(scatter_kernel, out_shape=[jax.ShapeDtypeStruct(s, F32) fo...  36.7 us
    pallas_call x1, Pallas kernels, back(): pl.pallas_call(back_kernel, out_shape=[jax.ShapeDtypeStruct((TOK, 1152),...  31 us
    pallas_call x1, Pallas kernels, tokens_sum(): pl.pallas_call(tokens_sum_kernel, out_shape=[jax.ShapeDtypeStruct(rows, F...  23.2 us
    dot_general x5, matrix products, dot_t(): lax.dot_general(a, b, (((1,), (1,)), ((), ())), preferred_element_type=F32)  18.4 us
    dot_general x3, matrix products, dot(): return jnp.dot(a, b, preferred_element_type=F32)  8.49 us
    dot_general x2, matrix products, t_dot(): lax.dot_general(a, b, (((0,), (0,)), ((), ())), preferred_element_type=F32)  6 us

profile of v1, /device:TPU:0, one launch (start us, length us, event | category | flops | bytes accessed | tf_op | source)
XLA Modules:
  0.0 233.1 jit_solution(12658210620133517069)
XLA Ops:
  0.7 1.3 maximum_bitcast_fusion.vec
  2.0 1.1 fusion.29
  3.1 0.6 broadcast_in_dim_tile.3.freq
  3.7 1.4 copy.35.pos
  5.1 82.5 %forward.1 = (bf16[4,4,2,32,1152]{4,3,2,1,0:T(8,128)(2,1)}, bf16[4,4,2,32,896]{4,3,2,1,0:T(8,128)(2,1)}, bf16[4,4,2,48,896]{4,3,2,1,0:T(8,128)(2,1)}, bf16[4,4,2...) custom-call(bf16[28,896]{1,0:T(8,128)(2,1)} %q.1, ...), custom_call_target="tpu_custom_call" | custom-call | tf_op jit(solution)/shard_map/forward/pallas_call | solution.py:433
  87.6 0.8 slice_reduce_fusion.1
  88.4 1.3 multiply_reduce_fusion.2
  89.7 2.6 %fusion.12.mid = bf16[512,1024]{1,0:T(8,128)(2,1)S(1)} fusion(bf16[512,896]{1,0:T(8,128)(2,1)} %bitcast.62, s32[896]{0:T(1024)S(1)} %get-tuple-element.93), kind=kOutput, calls=%fused_computation.20 | convolution fusion | flops 940965888 | bytes 1969664 | tf_op jit(solution)/shard_map/dot_general | solution.py:922
  92.4 1.8 fusion.56
  94.2 0.3 copy-done.1
  94.5 0.2 copy-done.6
  94.7 1.8 fusion.55
  96.6 0.1 copy-done.10
  96.6 4.1 %multiply_convert_fusion = (bf16[512,1536]{1,0:T(8,128)(2,1)}, bf16[512,1536]{1,0:T(8,128)(2,1)S(1)}, bf16[512,1536]{1,0:T(8,128)(2,1)S(1)}) fusion(f32[512,1536]{1,0:T(8,128)S(1)} %fusion.56, f32[512,1536]{1,0:T(8,128)S(1)} %fusion.55, bf16[512,1024]{1,0:T(8,128)(2,1)S(1)} %fusion.12.mid, bf16[1024,1536]{1,0:T(8,128)(2,1)S(1)} %bitcast.57), kind=kOutput, calls=%fused_computation.9 | convolution fusion | flops 1623195648 | bytes 15204352 | tf_op jit(solution)/shard_map/dot_general | solution.py:922
  100.7 3.2 %fusion.57 = f32[512,1024]{1,0:T(8,128)} fusion(bf16[512,1536]{1,0:T(8,128)(2,1)S(1)} %get-tuple-element.84.gg, bf16[1024,1536]{1,0:T(8,128)(2,1)S(1)} %bitcast.59), kind=kOutput, calls=%fused_computation.95 | convolution fusion | flops 1610612736 | bytes 6815744 | tf_op jit(solution)/shard_map/dot_general | solution.py:926
  103.9 0.0 copy-done.4
  103.9 6.5 %fusion.13 = bf16[512,896]{1,0:T(8,128)(2,1)} fusion(s32[896]{0:T(1024)S(1)} %get-tuple-element.93, f32[512,1024]{1,0:T(8,128)} %fusion.57, bf16[512,1536]{1,0:T(8,128)(2,1)S(1)} %get-tuple-element.85.gu, bf16[1024,1536]{1,0:T(8,128)(2,1)} %bitcast.56), kind=kOutput, calls=%fused_computation.21 | convolution fusion | flops 2552561664 | bytes 7736832 | tf_op jit(solution)/shard_map/dot_general | solution.py:926
  110.4 23.2 %scatter_tokens.1 = (f32[128,896]{1,0:T(8,128)}, bf16[4,128,896]{2,1,0:T(8,128)(2,1)}, bf16[4,4,48,896]{3,2,1,0:T(8,128)(2,1)}, bf16[4,4,32,768]{3,2,1,0:T(8,128...) custom-call(bf16[4,128,896]{2,1,0:T(8,128)(2,1)} %bitcast.52, ...), custom_call_target="tpu_custom_call" | custom-call | tf_op jit(solution)/shard_map/scatter_tokens/pallas_call | solution.py:706
  133.6 1.3 multiply_reduce_fusion
  134.8 0.1 fusion.54
  134.9 0.1 pad_maximum_fusion.1
  135.0 1.2 multiply_add_fusion
  136.2 3.5 %fusion.17.grad = bf16[128,896]{1,0:T(8,128)(2,1)} fusion(s32[896]{0:T(1024)S(1)} %get-tuple-element.93, bf16[1024,896]{1,0:T(8,128)(2,1)} %bitcast.61, f32[128,896]{1,0:T(8,128)S(1)} %multiply_add_fusion), kind=kOutput, calls=%fused_computation.27 | convolution fusion | flops 471040000 | bytes 2526720 | tf_op jit(solution)/shard_map/dot_general | solution.py:926
  139.7 31.0 %attention_backward.1 = (bf16[128,1152]{1,0:T(8,128)(2,1)}, bf16[4,48,896]{2,1,0:T(8,128)(2,1)}, bf16[4,32,768]{2,1,0:T(8,128)(2,1)}, bf16[4,32,1536]{2,1,0:T(8,128)(2,1)}, bf16[4,32,768]{2,1,0:T(8,128)(2,1)}) custom-call(bf16[128,896]{1,0:T(8,128)(2,1)} %get-tuple-element.47.q, bf16[128,896]{1,0:T(8,128)(2,1)} %fusion.17.grad, ...), custom_call_target="tpu_custom_call" | custom-call | tf_op jit(solution)/shard_map/attention_backward/pallas_call | solution.py:590
  170.8 3.4 %fusion.24 = (f32[128]{0:T(128)S(1)}, bf16[896]{0:T(1024)(128)(2,1)S(1)}, f32[128,896]{1,0:T(8,128)S(1)}) fusion(bf16[128,896]{1,0:T(8,128)(2,1)S(1)} %copy-done.2, f32[896]{0:T(1024)S(1)} %get-tuple-element.81, f32[128]{0:T(128)S(1)} %add_rsqrt_fusion.1, s32[896]{0:T(1024)S(1)} %get-tuple-element.93, bf16[128,1152]{1,0:T(8,128)(2,1)} %get-tuple-element.63, ...), kind=kOutput, calls=%fused_computation.36 | convolution fusion | flops 538721280 | bytes 3352320 | tf_op jit(solution)/shard_map/dot_general | solution.py:926
  174.2 0.9 fusion.28
  175.1 2.9 %select_convert_fusion = bf16[1024,896]{1,0:T(8,128)(2,1)} fusion(bf16[896]{0:T(1024)(128)(2,1)S(1)} %pad_maximum_fusion.1, bf16[896]{0:T(1024)(128)(2,1)S(1)} %get-tuple-element.80, s32[896]{0:T(1024)S(1)} %get-tuple-element.94, s32[1024]{0:T(1024)S(1)} %add_select_fusion, pred[1024]{0:T(1024)(128)(4,1)S(1)} %fusion.40, bf16[128,896]{1,0:T(8,128)(2,1)S(1)} %copy-done.8, ...), kind=kOutput, calls=%fused_computation.1 | convolution fusion | flops 473677824 | bytes 2539008 | tf_op jit(solution)/shard_map/dot_general | solution.py:930
  177.9 3.1 %convolution_convert_fusion = bf16[1024,1152]{1,0:T(8,128)(2,1)} fusion(bf16[128,1152]{1,0:T(8,128)(2,1)S(1)} %copy-done.12, s32[896]{0:T(1024)S(1)} %get-tuple-element.93, f32[1024]{0:T(1024)S(1)} %fusion.49, bf16[128,896]{1,0:T(8,128)(2,1)S(1)} %copy-done.2, f32[896]{0:T(1024)S(1)} %get-tuple-element.81, f32[128]{0:T(128)S(1)} %add_rsqrt_fusion.1), kind=kOutput, calls=%fused_computation | convolution fusion | flops 539688960 | bytes 2895360 | tf_op jit(solution)/shard_map/dot_general | solution.py:930
  181.1 36.7 %scatter_grads.1 = (f32[8,1152]{1,0:T(8,128)}, f32[8,896]{1,0:T(8,128)}, f32[48,896]{1,0:T(8,128)}, f32[4,8,768]{2,1,0:T(8,128)}, f32[4,8,1536]{2,1,0:T(8,128)},...) custom-call(bf16[4,4,2,32,1152]{4,3,2,1,0:T(8,128)(2,1)} %bitcast.48, bf16[4,4,2,32,896]{4,3,2,1,0:T(8,128)(2,1)} %bitcast.49, ...), custom_call_target="tpu_custom_call" | custom-call | tf_op jit(solution)/shard_map/scatter_grads/pallas_call | solution.py:896
  217.8 1.8 add_convert_fusion.1
  219.6 1.0 copy.37
  220.6 0.8 slice.53
  221.4 0.6 fusion.52
  221.9 0.8 slice.55
  222.7 0.6 constant_dynamic-slice_fusion.1
  223.3 0.6 fusion.51
  223.9 1.3 fusion.53
  225.2 1.4 slice.54
  226.5 1.6 slice.63
  228.1 1.0 pad_maximum_fusion
  229.1 0.1 copy.39
  229.2 0.2 reshape.219
  229.5 0.3 copy.40
  229.8 1.1 reshape.220
  230.9 0.2 reshape.217
  231.1 0.3 copy.38
  231.4 1.1 reshape.218
  232.5 0.6 copy.42
  (34 shorter events, 0.2 us)
Async XLA Ops:
  88.4 3.9 %copy-start.11 = (bf16[4,4,2,32,1536]{4,3,2,1,0:T(8,128)(2,1)S(1)}, bf16[4,4,2,32,1536]{4,3,2,1,0:T(8,128)(2,1)}, u32[]{:S(2)}) copy-start(bf16[4,4,2,32,1536]{4,3,2,1,0:T(8,128)(2,1)} %get-tuple-element.52) | copy-start | bytes 9437188
  92.3 4.2 %copy-start.5 = (bf16[512,1024]{1,0:T(8,128)(2,1)}, bf16[512,1024]{1,0:T(8,128)(2,1)S(1)}, u32[]{:S(2)}) copy-start(bf16[512,1024]{1,0:T(8,128)(2,1)S(1)} %fusion.12.mid) | copy-start | bytes 3145732
  92.3 2.2 copy-start.1
  92.3 2.4 %copy-start.6 = (bf16[4,128,896]{2,1,0:T(8,128)(2,1)S(1)}, bf16[4,128,896]{2,1,0:T(8,128)(2,1)}, u32[]{:S(2)}) copy-start(bf16[4,128,896]{2,1,0:T(8,128)(2,1)} %get-tuple-element.48) | copy-start | bytes 2752516
  94.7 1.9 copy-start.10
  100.7 3.2 %copy-start.3 = (bf16[512,1536]{1,0:T(8,128)(2,1)}, bf16[512,1536]{1,0:T(8,128)(2,1)S(1)}, u32[]{:S(2)}) copy-start(bf16[512,1536]{1,0:T(8,128)(2,1)S(1)} %get-tuple-element.84.gg) | copy-start | bytes 4718596
  100.7 3.2 %copy-start.4 = (bf16[512,1536]{1,0:T(8,128)(2,1)}, bf16[512,1536]{1,0:T(8,128)(2,1)S(1)}, u32[]{:S(2)}) copy-start(bf16[512,1536]{1,0:T(8,128)(2,1)S(1)} %get-tuple-element.85.gu) | copy-start | bytes 4718596
  110.4 23.2 %copy-start = (f32[128,896]{1,0:T(8,128)S(1)}, f32[128,896]{1,0:T(8,128)}, u32[]{:S(2)}) copy-start(f32[128,896]{1,0:T(8,128)} %get-tuple-element.45) | copy-start | bytes 1376260
  110.4 24.6 %copy-start.7 = (bf16[128,896]{1,0:T(8,128)(2,1)S(1)}, bf16[128,896]{1,0:T(8,128)(2,1)}, u32[]{:S(2)}) copy-start(bf16[128,896]{1,0:T(8,128)(2,1)} %t.1) | copy-start | bytes 688132
  139.7 31.1 %copy-start.2 = (bf16[128,896]{1,0:T(8,128)(2,1)S(1)}, bf16[128,896]{1,0:T(8,128)(2,1)}, u32[]{:S(2)}) copy-start(bf16[128,896]{1,0:T(8,128)(2,1)} %block.1) | copy-start | bytes 688132
  170.8 4.3 %copy-start.8 = (bf16[128,896]{1,0:T(8,128)(2,1)S(1)}, bf16[128,896]{1,0:T(8,128)(2,1)}, u32[]{:S(2)}) copy-start(bf16[128,896]{1,0:T(8,128)(2,1)} %get-tuple-element.55.att) | copy-start | bytes 688132
  175.1 2.9 %copy-start.12 = (bf16[128,1152]{1,0:T(8,128)(2,1)S(1)}, bf16[128,1152]{1,0:T(8,128)(2,1)}, u32[]{:S(2)}) copy-start(bf16[128,1152]{1,0:T(8,128)(2,1)} %get-tuple-element.63) | copy-start | bytes 884740
  229.2 3.3 %copy-start.9 = (f32[8,896]{1,0:T(8,128)S(1)}, f32[8,896]{1,0:T(8,128)}, u32[]{:S(2)}) copy-start(f32[8,896]{1,0:T(8,128)} %get-tuple-element.71) | copy-start | bytes 86020

commit v2 on v1

--- a/solution.py
+++ b/solution.py
@@ -3,6 +3,7 @@
 
 import jax
 import jax.numpy as jnp
+import numpy as np
 from jax import lax
 from jax.experimental import pallas as pl
 from jax.experimental.pallas import tpu as pltpu
@@ -227,9 +228,9 @@
 
 
 def forward_kernel(q, kw, v, o, down, gate, up, vec, t, block, pos, freq, *refs):
-    ao, oo, do, go, uo, to, mo, seen, qo, att, logs, mid, gains, turn = refs[:14]
+    a_out, o_out, do, go, uo, to, mo, seen, qo, att, logs, mid, gains, turn = refs[:14]
     wq, wk, wv, wo, wd, wg, wu, units, own_a, own_o, own_d, own_g, own_u = refs[14:27]
-    spread, kv, low, qs, os, send, recv, load, loc = refs[27:]
+    spread, kv, low, qs, os, ao, oo, send, recv, load, loc = refs[27:]
     z, x, k, c = place()
     f = lax.axis_index("fsdp")
     me = f * 4 + c
@@ -357,6 +358,12 @@
         copy.wait()
     for copy in third:
         copy.wait_recv()
+    stores = [
+        pltpu.make_async_copy(ao, a_out, loc.at[6]),
+        pltpu.make_async_copy(oo, o_out, loc.at[7]),
+    ]
+    for copy in stores:
+        copy.start()
     for ring in line:
         ring.near()
         ring.far()
@@ -406,7 +413,8 @@
     factor = lax.rsqrt(jnp.mean(middle * middle, axis=-1, keepdims=True) + EPSILON)
     low[...] = (middle * factor * both[1:2]).astype(BF)
     mid_ring = RingGather(cp, lambda p, h: mo.at[p, rows[h]], lambda h: low.at[rows[h]], c, *ys)
-    mo[c] = low[...]
+    stores.append(pltpu.make_async_copy(low, mo.at[c], loc.at[8]))
+    stores[2].start()
     for ring in plane:
         ring.near()
         ring.far()
@@ -419,6 +427,8 @@
     mid_ring.far()
     for copy in last:
         copy.wait_recv()
+    for copy in stores:
+        copy.wait()
     cp.finish()
 
 
@@ -445,7 +455,7 @@
             jax.ShapeDtypeStruct((2, TOK, 128), F32),
         ],
         in_specs=[HBM] * 7 + [VMEM] + [HBM] + [VMEM] * 3,
-        out_specs=[VMEM] * 14,
+        out_specs=[HBM] * 7 + [VMEM] * 7,
         scratch_shapes=[pltpu.VMEM(w.shape, BF) for w in weights]
         + [pltpu.VMEM((2432, 16 * UP), BF)]
         + [pltpu.VMEM(p, BF) for p in packed]
@@ -455,10 +465,12 @@
             pltpu.VMEM((TOK, D), BF),
             pltpu.VMEM((HEADS, TOK, 128), BF),
             pltpu.VMEM((HEADS, TOK, 128), BF),
+            pltpu.VMEM((4, 4, 2) + packed[0], BF),
+            pltpu.VMEM((4, 4, 2) + packed[1], BF),
             pltpu.SemaphoreType.DMA((count,)),
             pltpu.SemaphoreType.DMA((count,)),
             pltpu.SemaphoreType.DMA((7,)),
-            pltpu.SemaphoreType.DMA((6,)),
+            pltpu.SemaphoreType.DMA((9,)),
         ],
         compiler_params=pltpu.CompilerParams(
             collective_id=0, has_side_effects=True, vmem_limit_bytes=VMEM_FORWARD
@@ -637,7 +649,7 @@
     return [pltpu.VMEM(half, BF), pltpu.VMEM(half, BF), pltpu.VMEM((2,) + rows, BF)]
 
 
-def tokens_sum_kernel(t, hidden, cot, mid, gg, gu, wd, out, part, *refs):
+def tokens_sum_kernel(*refs):
     n = len(PIECES)
 
     def take(count):
@@ -645,13 +657,19 @@
         head, refs = refs[:count], refs[count:]
         return head
 
-    sums, full, got = take(n), take(3), take(n)
-    acc, far, near, send, recv = refs
+    ins, (out, part_out), sums = take(7), take(2), take(n)
+    loaded, full, got = take(7), take(3), take(n)
+    part, acc, far, near, send, recv, load, store = refs
+    t, hidden, cot, mid, gg, gu, wd = loaded
     z, x, k, c = place()
     ys = [device(z, x, k, plus(c, i)) for i in (1, 3)]
     sibling = device(z, x, 1 - k, c)
+    loads = [pltpu.make_async_copy(ins[i], loaded[i], load.at[i]) for i in range(7)]
+    for copy in loads:
+        copy.start()
     greet(ys + [sibling])
     cp = Copies(send, recv)
+    loads[0].wait()
     ring = tokens_ring(cp, t, acc, far, near, c, ys)
     ring.plain()
     firsts = {}
@@ -672,9 +690,14 @@
                 src = full[m].at[:, :, 1 - k, :, pl.ds(first, count)]
                 firsts[j] = cp.go(src, got[j], sibling)
 
+    loads[1].wait()
+    loads[2].wait()
     product(0, hidden, cot)
     ring.forward()
+    loads[3].wait()
+    loads[4].wait()
     product(1, mid, gg)
+    loads[5].wait()
     product(2, mid, gu)
     ring.finish()
     out[...] = t[c].astype(F32) + near[0].astype(F32) + near[1].astype(F32)
@@ -684,7 +707,10 @@
         part[i] = dot(hidden[rows], wd[...]).astype(BF)
         return carry
 
+    loads[6].wait()
     lax.fori_loop(0, 4, down, 0)
+    stores = [pltpu.make_async_copy(part, part_out, store.at[n])]
+    stores[0].start()
     for j in (0, 2, 1, 3):
         a, _, first, count, _ = PIECES[j]
         firsts[j].wait_recv()
@@ -692,10 +718,15 @@
         def add(i, carry, j=j, a=a, first=first, count=count):
             at = (i // 4, i % 4)
             mine = full[a][at + (k, slice(None), slice(first, first + count))]
-            sums[j][at] = (mine.astype(F32) + got[j][at].astype(F32)).astype(BF)
+            got[j][at] = (mine.astype(F32) + got[j][at].astype(F32)).astype(BF)
             return carry
 
         lax.fori_loop(0, 16, add, 0)
+        copy = pltpu.make_async_copy(got[j], sums[j], store.at[j])
+        copy.start()
+        stores.append(copy)
+    for copy in stores:
+        copy.wait()
     cp.finish()
 
 
@@ -707,12 +738,19 @@
         tokens_sum_kernel,
         out_shape=[jax.ShapeDtypeStruct(rows, F32), jax.ShapeDtypeStruct(t.shape, BF)]
         + [jax.ShapeDtypeStruct((4, 4) + s, BF) for s in shapes],
-        in_specs=[VMEM] * 7,
-        out_specs=[VMEM] * (n + 2),
-        scratch_shapes=[pltpu.VMEM((4, 4, 2) + s, BF) for s in FFN]
+        in_specs=[HBM] * 7,
+        out_specs=[VMEM] + [HBM] * (n + 1),
+        scratch_shapes=[pltpu.VMEM(s.shape, BF) for s in (t, hidden, cot, mid, gg, gu, wd)]
+        + [pltpu.VMEM((4, 4, 2) + s, BF) for s in FFN]
         + [pltpu.VMEM((4, 4) + s, BF) for s in shapes]
+        + [pltpu.VMEM(t.shape, BF)]
         + tokens_scratch(rows)
-        + [pltpu.SemaphoreType.DMA((6 + n,)), pltpu.SemaphoreType.DMA((6 + n,))],
+        + [
+            pltpu.SemaphoreType.DMA((6 + n,)),
+            pltpu.SemaphoreType.DMA((6 + n,)),
+            pltpu.SemaphoreType.DMA((7,)),
+            pltpu.SemaphoreType.DMA((n + 1,)),
+        ],
         compiler_params=pltpu.CompilerParams(
             collective_id=4, has_side_effects=True, vmem_limit_bytes=58 * 1024 * 1024
         ),
@@ -720,7 +758,7 @@
     )(t, hidden, cot, mid, gg, gu, wd)
 
 
-def scatter_kernel(a, o, p0, p1, p2, p3, t, *refs):
+def scatter_kernel(a, o, p0, p1, p2, p3, t, mid, *refs):
     n = len(PIECES)
 
     def take(count):
@@ -728,7 +766,7 @@
         head, refs = refs[:count], refs[count:]
         return head
 
-    outs, (t_out,) = take(2 + n), take(1)
+    (q_out, k_out, v_out, a_vec, o_out, o_vec, d_out), outs, (t_out,) = take(7), take(n - 1), take(1)
     own, got1, far2, near2, sum2 = (take(2) for _ in range(5))
     line = sum2 + take(n)
     far3, near3, fins, gots = take(2 + n), take(2 + n), take(2 + n), take(2)
@@ -797,14 +835,14 @@
         total = line[m][x if ways[m] else z].astype(F32)
         total = total + near3[m][0].astype(F32) + near3[m][1].astype(F32)
         if m == 2:
-            outs[m][...] = total
+            d_out[...] = total[:UN]
             return
         fins[m][...] = total.reshape(fins[m].shape)
         for i in (1, 2, 3):
-            target = gots[m].at[i - 1] if m < 2 else outs[m].at[c]
+            target = gots[m].at[i - 1] if m < 2 else outs[m - 3].at[c]
             closing[m, i] = cp.go(fins[m].at[plus(c, i)], target, ys[i - 1])
         if m > 2:
-            outs[m][c] = fins[m][c]
+            outs[m - 3][c] = fins[m][c]
 
     def join(m, i):
         p = spot(m, i)
@@ -859,25 +897,34 @@
     for m in range(2):
         third[m].forward()
     tokens.finish()
-    t_out[...] = t[c].astype(F32) + near[0].astype(F32) + near[1].astype(F32)
+    total = t[c].astype(F32) + near[0].astype(F32) + near[1].astype(F32)
+    t_out[...] = (mid[...] + total).astype(BF)
     for m in range(2):
         close(m)
     for copy in closing.values():
         copy.wait_recv()
+    joined = []
     for m in range(2):
         total = fins[m][c]
         for i in range(3):
             total = total + gots[m][i]
-        outs[m][...] = total
+        joined.append(total)
+    q_out[...] = joined[0][:7, :896]
+    k_out[...] = joined[0][:7, 896:1024]
+    v_out[...] = joined[0][:7, 1024:]
+    a_vec[...] = joined[0][7:]
+    o_out[...] = joined[1][:7]
+    o_vec[...] = joined[1][7:]
     cp.finish()
 
 
-def scatter(a, o, sums, t):
+def scatter(a, o, sums, t, mid):
     n = len(PIECES)
     pair = [a.shape[3:], o.shape[3:]]
     shapes = pair + [s.shape[1:] for s in sums]
     quarter = [(s[0] // 4, s[1]) for s in shapes]
-    outs = quarter[:2] + [shapes[2]] + [(4,) + q for q in quarter[3:]]
+    outs = [(7, 896), (7, 128), (7, 128), (1, 1152), (7, D), (1, D), (UN, D)]
+    outs += [(4,) + q for q in quarter[3:]]
     scratch = []
     for lead in ((4, 4), (4, 4), (2, 2), (2, 4)):
         scratch += [pltpu.VMEM(lead + s, BF) for s in pair]
@@ -896,15 +943,15 @@
     return pl.pallas_call(
         scatter_kernel,
         out_shape=[jax.ShapeDtypeStruct(s, F32) for s in outs]
-        + [jax.ShapeDtypeStruct(t.shape[1:], F32)],
-        in_specs=[ANY] * (2 + n) + [VMEM],
-        out_specs=[VMEM] * (3 + n),
+        + [jax.ShapeDtypeStruct(t.shape[1:], BF)],
+        in_specs=[ANY] * (2 + n) + [VMEM] * 2,
+        out_specs=[VMEM] * (7 + n),
         scratch_shapes=scratch,
         compiler_params=pltpu.CompilerParams(
             collective_id=5, has_side_effects=True, vmem_limit_bytes=58 * 1024 * 1024
         ),
         name="scatter_grads",
-    )(a, o, *sums, t)
+    )(a, o, *sums, t, mid)
 
 
 def norm_forward(values):
@@ -958,7 +1005,7 @@
     spread = choose((i896 + i896 // 7)[:, None] == jnp.arange(DP)[None, :])
 
     half = HEAD_SIZE // 2
-    frequency = ROTARY_BASE ** (-(jnp.arange(half, dtype=F32) * 2.0 / HEAD_SIZE))
+    frequency = ROTARY_BASE ** (-(np.arange(half) * 2.0 / HEAD_SIZE))
     places = positions[:, None]
     (
         all_a,
@@ -989,7 +1036,7 @@
         cotangent,
         block_input,
         places,
-        jnp.tile(frequency, 4)[None],
+        jnp.asarray(np.tile(frequency, 4)[None], F32),
     )
     gain_first, gain_second = gains[0], gains[1]
     all_a = all_a.reshape(DP, 1152)
@@ -1040,14 +1087,14 @@
         i896[None, :] // 7 == group, grad_gain_one[None, :], jnp.roll(grad_gain_two, 448)[None, :]
     )
     grad_output_w = jnp.where(jnp.arange(DP)[:, None] % 8 == 7, gains, grad_output_w)
-    sum_a, sum_o, sum_d, sum_u0, sum_g, sum_u1, out_sum = scatter(
+    sum_q, sum_k, sum_v, vec_a, sum_o, vec_o, sum_d, sum_u0, sum_g, sum_u1, block_output = scatter(
         grad_qkv_w.astype(BF).reshape(4, 4, 2, 32, 1152),
         grad_output_w.astype(BF).reshape(4, 4, 2, 32, D),
         sums,
         out_part,
+        residual_mid,
     )
     sum_u = jnp.concatenate([sum_u0, sum_u1], axis=2)
-    block_output = (residual_mid + out_sum).astype(BF)
 
     def columns(parts):
         parts = parts[:, :7].reshape(4, 7, 32, UP)[..., :UN]
@@ -1057,17 +1104,17 @@
     return (
         block_output,
         grad_input,
-        lax.dynamic_slice(sum_o[7], (at,), (7,)),
-        sum_a[:7, :896],
-        lax.dynamic_slice(sum_a[7], (at,), (7,)),
-        sum_a[:7, 896:1024],
-        sum_a[:7, 1024:1152],
-        lax.dynamic_slice(sum_a[7], (1024 + stretch,), (1,)),
-        sum_o[:7],
-        lax.dynamic_slice(sum_o[7], (lax.rem(at + 448, 896),), (7,)),
+        lax.dynamic_slice(vec_o[0], (at,), (7,)),
+        sum_q,
+        lax.dynamic_slice(vec_a[0], (at,), (7,)),
+        sum_k,
+        sum_v,
+        lax.dynamic_slice(vec_a[0], (1024 + stretch,), (1,)),
+        sum_o,
+        lax.dynamic_slice(vec_o[0], (lax.rem(at + 448, 896),), (7,)),
         columns(sum_g),
         columns(sum_u),
-        sum_d[:UN],
+        sum_d,
     )
 
 

time: 234 us -> 221 us (0.944)
  Pallas kernels: 173 us -> 165 us
    slice x5 -> x0, local copies, waits for them, and re-layouts: 5.73 us -> none  [the longest x1 1.58 us: local(): sum_d[:UN]]
    pallas_call x1, Pallas kernels: 23.2 us -> 18.4 us  [tokens_sum(): pl.pallas_call(tokens_sum_kernel, out_shape=[jax.ShapeDtypeStruct(rows, F...]
    pallas_call x1, Pallas kernels: 82.5 us -> 78.8 us  [forward(): pl.pallas_call(forward_kernel, out_shape=[out(*p) for p in packed] + [gro...]
    unnamed x27 -> x44, local copies, waits for them, and re-layouts: 1.28 us -> 4.44 us
where the time goes in v2:
time: 221 us
  Pallas kernels  165 us (75%)
  matrix products  31.4 us (14%)
  local copies, waits for them, and re-layouts  14.9 us (7%)
  other arithmetic  8.08 us (4%)
    pallas_call x1, Pallas kernels, forward(): pl.pallas_call(forward_kernel, out_shape=[out(*p) for p in packed] + [gro...  78.8 us
    pallas_call x1, Pallas kernels, scatter(): pl.pallas_call(scatter_kernel, out_shape=[jax.ShapeDtypeStruct(s, F32) fo...  37.2 us
    pallas_call x1, Pallas kernels, back(): pl.pallas_call(back_kernel, out_shape=[jax.ShapeDtypeStruct((TOK, 1152),...  30.9 us
    pallas_call x1, Pallas kernels, tokens_sum(): pl.pallas_call(tokens_sum_kernel, out_shape=[jax.ShapeDtypeStruct(rows, F...  18.4 us
    dot_general x5, matrix products, dot_t(): lax.dot_general(a, b, (((1,), (1,)), ((), ())), preferred_element_type=F32)  16.9 us
    dot_general x3, matrix products, dot(): return jnp.dot(a, b, preferred_element_type=F32)  8.47 us
    dot_general x2, matrix products, t_dot(): lax.dot_general(a, b, (((0,), (0,)), ((), ())), preferred_element_type=F32)  6.01 us
    unnamed x44, local copies, waits for them, and re-layouts  4.44 us

profile of v2, /device:TPU:0, one launch (start us, length us, event | category | flops | bytes accessed | tf_op | source)
XLA Modules:
  0.0 220.7 jit_solution(8296792481441747096)
XLA Ops:
  0.7 1.3 maximum_bitcast_fusion.vec
  2.0 1.1 fusion.29
  3.1 1.4 copy.36.pos
  4.5 78.8 %forward.1 = (bf16[4,4,2,32,1152]{4,3,2,1,0:T(8,128)(2,1)}, bf16[4,4,2,32,896]{4,3,2,1,0:T(8,128)(2,1)}, bf16[4,4,2,48,896]{4,3,2,1,0:T(8,128)(2,1)}, bf16[4,4,2...) custom-call(bf16[28,896]{1,0:T(8,128)(2,1)} %q.1, ...), custom_call_target="tpu_custom_call" | custom-call | tf_op jit(solution)/shard_map/forward/pallas_call | solution.py:443
  83.3 0.8 slice_reduce_fusion.1
  84.1 1.3 multiply_reduce_fusion.2
  85.4 2.6 %fusion.12.refs_3_ = bf16[512,1024]{1,0:T(8,128)(2,1)S(1)} fusion(bf16[512,896]{1,0:T(8,128)(2,1)} %bitcast.60, s32[896]{0:T(1024)S(1)} %get-tuple-element.99), kind=kOutput, calls=%fused_computation.20 | convolution fusion | flops 940965888 | bytes 1969664 | tf_op jit(solution)/shard_map/dot_general | solution.py:969
  88.1 1.8 fusion.55
  89.9 0.3 copy-done.1
  90.2 0.2 copy-done.6
  90.4 1.8 fusion.54
  92.2 0.0 copy-done.5
  92.3 0.1 copy-done.15
  92.3 4.1 %multiply_convert_fusion = (bf16[512,1536]{1,0:T(8,128)(2,1)}, bf16[512,1536]{1,0:T(8,128)(2,1)S(1)}, bf16[512,1536]{1,0:T(8,128)(2,1)S(1)}) fusion(f32[512,1536]{1,0:T(8,128)S(1)} %fusion.55, f32[512,1536]{1,0:T(8,128)S(1)} %fusion.54, bf16[512,1024]{1,0:T(8,128)(2,1)S(1)} %fusion.12.refs_3_, bf16[1024,1536]{1,0:T(8,128)(2,1)S(1)} %bitcast.55), kind=kOutput, calls=%fused_computation.9 | convolution fusion | flops 1623195648 | bytes 15204352 | tf_op jit(solution)/shard_map/dot_general | solution.py:969
  96.4 3.2 %fusion.56 = f32[512,1024]{1,0:T(8,128)} fusion(bf16[512,1536]{1,0:T(8,128)(2,1)S(1)} %get-tuple-element.92.refs_4_, bf16[1024,1536]{1,0:T(8,128)(2,1)S(1)} %bitcast.57), kind=kOutput, calls=%fused_computation.92 | convolution fusion | flops 1610612736 | bytes 6815744 | tf_op jit(solution)/shard_map/dot_general | solution.py:973
  99.6 0.0 copy-done.4
  99.6 6.5 %fusion.13 = bf16[512,896]{1,0:T(8,128)(2,1)} fusion(s32[896]{0:T(1024)S(1)} %get-tuple-element.99, f32[512,1024]{1,0:T(8,128)} %fusion.56, bf16[512,1536]{1,0:T(8,128)(2,1)S(1)} %get-tuple-element.93.refs_5_, bf16[1024,1536]{1,0:T(8,128)(2,1)} %bitcast.54), kind=kOutput, calls=%fused_computation.21 | convolution fusion | flops 2552561664 | bytes 7736832 | tf_op jit(solution)/shard_map/dot_general | solution.py:973
  106.1 18.4 %scatter_tokens.1 = (f32[128,896]{1,0:T(8,128)}, bf16[4,128,896]{2,1,0:T(8,128)(2,1)}, bf16[4,4,48,896]{3,2,1,0:T(8,128)(2,1)}, bf16[4,4,32,768]{3,2,1,0:T(8,128...) custom-call(bf16[4,128,896]{2,1,0:T(8,128)(2,1)} %bitcast.51, ...), custom_call_target="tpu_custom_call" | custom-call | tf_op jit(solution)/shard_map/scatter_tokens/pallas_call | solution.py:737
  124.5 0.0 copy-done
  124.5 1.3 multiply_reduce_fusion
  125.8 0.1 fusion.53
  125.8 0.1 pad_maximum_fusion.1
  125.9 1.2 multiply_add_fusion
  127.1 2.0 fusion.17.grad
  129.2 30.9 %attention_backward.1 = (bf16[128,1152]{1,0:T(8,128)(2,1)}, bf16[4,48,896]{2,1,0:T(8,128)(2,1)}, bf16[4,32,768]{2,1,0:T(8,128)(2,1)}, bf16[4,32,1536]{2,1,0:T(8,128)(2,1)}, bf16[4,32,768]{2,1,0:T(8,128)(2,1)}) custom-call(bf16[128,896]{1,0:T(8,128)(2,1)} %get-tuple-element.50.q, bf16[128,896]{1,0:T(8,128)(2,1)} %fusion.17.grad, ...), custom_call_target="tpu_custom_call" | custom-call | tf_op jit(solution)/shard_map/attention_backward/pallas_call | solution.py:602
  160.1 3.4 %fusion.24 = (f32[128]{0:T(128)S(1)}, bf16[896]{0:T(1024)(128)(2,1)S(1)}, f32[128,896]{1,0:T(8,128)S(1)}) fusion(bf16[128,896]{1,0:T(8,128)(2,1)S(1)} %copy-done.2, f32[896]{0:T(1024)S(1)} %get-tuple-element.89, f32[128]{0:T(128)S(1)} %add_rsqrt_fusion.1, s32[896]{0:T(1024)S(1)} %get-tuple-element.99, bf16[128,1152]{1,0:T(8,128)(2,1)} %get-tuple-element.67, ...), kind=kOutput, calls=%fused_computation.36 | convolution fusion | flops 538721280 | bytes 3352320 | tf_op jit(solution)/shard_map/dot_general | solution.py:973
  163.5 0.9 fusion.28
  164.4 2.9 %select_convert_fusion = bf16[1024,896]{1,0:T(8,128)(2,1)} fusion(bf16[896]{0:T(1024)(128)(2,1)S(1)} %pad_maximum_fusion.1, bf16[896]{0:T(1024)(128)(2,1)S(1)} %get-tuple-element.88, s32[896]{0:T(1024)S(1)} %get-tuple-element.100, s32[1024]{0:T(1024)S(1)} %add_select_fusion, pred[1024]{0:T(1024)(128)(4,1)S(1)} %fusion.40, ...), kind=kOutput, calls=%fused_computation.1 | convolution fusion | flops 473677824 | bytes 2539008 | tf_op jit(solution)/shard_map/dot_general | solution.py:977
  167.3 3.1 %convolution_convert_fusion = bf16[1024,1152]{1,0:T(8,128)(2,1)} fusion(bf16[128,1152]{1,0:T(8,128)(2,1)S(1)} %copy-done.18, s32[896]{0:T(1024)S(1)} %get-tuple-element.99, f32[1024]{0:T(1024)S(1)} %fusion.49, bf16[128,896]{1,0:T(8,128)(2,1)S(1)} %copy-done.2, f32[896]{0:T(1024)S(1)} %get-tuple-element.89, f32[128]{0:T(128)S(1)} %add_rsqrt_fusion.1), kind=kOutput, calls=%fused_computation | convolution fusion | flops 539688960 | bytes 2895360 | tf_op jit(solution)/shard_map/dot_general | solution.py:977
  170.5 37.2 %scatter_grads.1 = (f32[7,896]{1,0:T(8,128)}, f32[7,128]{1,0:T(8,128)}, f32[7,128]{1,0:T(8,128)}, f32[1,1152]{1,0:T(1,128)}, f32[7,896]{1,0:T(8,128)}, /*index=5...) custom-call(bf16[4,4,2,32,1152]{4,3,2,1,0:T(8,128)(2,1)} %bitcast.47, ...), custom_call_target="tpu_custom_call" | custom-call | tf_op jit(solution)/shard_map/scatter_grads/pallas_call | solution.py:943
  207.6 1.2 constant_dynamic-slice_fusion.1
  208.8 1.2 fusion.51
  210.1 1.3 fusion.52
  211.3 1.0 copy.38
  212.4 1.0 pad_maximum_fusion
  213.3 0.1 copy.40
  213.5 0.2 reshape.213
  213.8 0.3 copy.41
  214.1 1.1 reshape.214
  215.2 0.2 reshape.211
  215.5 0.3 copy.39
  215.8 1.1 reshape.212
  216.9 0.7 copy.48
  217.6 0.6 copy.49
  218.2 0.6 copy.50
  218.8 0.6 copy.51
  219.4 0.6 copy.52
  220.0 0.7 copy.53
  (42 shorter events, 0.2 us)
Async XLA Ops:
  84.1 3.9 %copy-start.16 = (bf16[4,4,2,32,1536]{4,3,2,1,0:T(8,128)(2,1)S(1)}, bf16[4,4,2,32,1536]{4,3,2,1,0:T(8,128)(2,1)}, u32[]{:S(2)}) copy-start(bf16[4,4,2,32,1536]{4,3,2,1,0:T(8,128)(2,1)} %get-tuple-element.56) | copy-start | bytes 9437188
  88.0 4.2 %copy-start.5 = (bf16[512,1024]{1,0:T(8,128)(2,1)}, bf16[512,1024]{1,0:T(8,128)(2,1)S(1)}, u32[]{:S(2)}) copy-start(bf16[512,1024]{1,0:T(8,128)(2,1)S(1)} %fusion.12.refs_3_) | copy-start | bytes 3145732
  88.0 2.2 copy-start.1
  88.1 2.4 %copy-start.6 = (bf16[4,128,896]{2,1,0:T(8,128)(2,1)S(1)}, bf16[4,128,896]{2,1,0:T(8,128)(2,1)}, u32[]{:S(2)}) copy-start(bf16[4,128,896]{2,1,0:T(8,128)(2,1)} %get-tuple-element.52) | copy-start | bytes 2752516
  90.4 1.9 copy-start.15
  96.4 3.2 %copy-start.3 = (bf16[512,1536]{1,0:T(8,128)(2,1)}, bf16[512,1536]{1,0:T(8,128)(2,1)S(1)}, u32[]{:S(2)}) copy-start(bf16[512,1536]{1,0:T(8,128)(2,1)S(1)} %get-tuple-element.92.refs_4_) | copy-start | bytes 4718596
  96.4 3.2 %copy-start.4 = (bf16[512,1536]{1,0:T(8,128)(2,1)}, bf16[512,1536]{1,0:T(8,128)(2,1)S(1)}, u32[]{:S(2)}) copy-start(bf16[512,1536]{1,0:T(8,128)(2,1)S(1)} %get-tuple-element.93.refs_5_) | copy-start | bytes 4718596
  106.1 18.4 %copy-start = (f32[128,896]{1,0:T(8,128)S(1)}, f32[128,896]{1,0:T(8,128)}, u32[]{:S(2)}) copy-start(f32[128,896]{1,0:T(8,128)} %get-tuple-element.51.mid) | copy-start | bytes 1376260
  106.1 19.9 %copy-start.7 = (bf16[128,896]{1,0:T(8,128)(2,1)S(1)}, bf16[128,896]{1,0:T(8,128)(2,1)}, u32[]{:S(2)}) copy-start(bf16[128,896]{1,0:T(8,128)(2,1)} %t.1) | copy-start | bytes 688132
  106.1 21.1 %copy-start.17 = (bf16[4,4,2,32,896]{4,3,2,1,0:T(8,128)(2,1)S(1)}, bf16[4,4,2,32,896]{4,3,2,1,0:T(8,128)(2,1)}, u32[]{:S(2)}) copy-start(bf16[4,4,2,32,896]{4,3,2,1,0:T(8,128)(2,1)} %get-tuple-element.58) | copy-start | bytes 5505028
  129.2 31.0 %copy-start.2 = (bf16[128,896]{1,0:T(8,128)(2,1)S(1)}, bf16[128,896]{1,0:T(8,128)(2,1)}, u32[]{:S(2)}) copy-start(bf16[128,896]{1,0:T(8,128)(2,1)} %block.1) | copy-start | bytes 688132
  160.1 4.3 %copy-start.9 = (bf16[128,896]{1,0:T(8,128)(2,1)S(1)}, bf16[128,896]{1,0:T(8,128)(2,1)}, u32[]{:S(2)}) copy-start(bf16[128,896]{1,0:T(8,128)(2,1)} %get-tuple-element.59.att) | copy-start | bytes 688132
  164.4 2.9 %copy-start.18 = (bf16[128,1152]{1,0:T(8,128)(2,1)S(1)}, bf16[128,1152]{1,0:T(8,128)(2,1)}, u32[]{:S(2)}) copy-start(bf16[128,1152]{1,0:T(8,128)(2,1)} %get-tuple-element.67) | copy-start | bytes 884740
  213.5 3.4 %copy-start.8 = (bf16[128,896]{1,0:T(8,128)(2,1)S(1)}, bf16[128,896]{1,0:T(8,128)(2,1)}, u32[]{:S(2)}) copy-start(bf16[128,896]{1,0:T(8,128)(2,1)} %get-tuple-element.114) | copy-start | bytes 688132
  213.7 3.9 %copy-start.12 = (f32[7,896]{1,0:T(8,128)S(1)}, f32[7,896]{1,0:T(8,128)}, u32[]{:S(2)}) copy-start(f32[7,896]{1,0:T(8,128)} %get-tuple-element.117) | copy-start | bytes 75268
  213.7 4.5 %copy-start.14 = (f32[7,128]{1,0:T(8,128)S(1)}, f32[7,128]{1,0:T(8,128)}, u32[]{:S(2)}) copy-start(f32[7,128]{1,0:T(8,128)} %get-tuple-element.119) | copy-start | bytes 10756
  213.7 5.1 %copy-start.13 = (f32[7,128]{1,0:T(8,128)S(1)}, f32[7,128]{1,0:T(8,128)}, u32[]{:S(2)}) copy-start(f32[7,128]{1,0:T(8,128)} %get-tuple-element.120) | copy-start | bytes 10756
  213.7 5.6 %copy-start.11 = (f32[7,896]{1,0:T(8,128)S(1)}, f32[7,896]{1,0:T(8,128)}, u32[]{:S(2)}) copy-start(f32[7,896]{1,0:T(8,128)} %get-tuple-element.122) | copy-start | bytes 75268
  213.7 6.2 %copy-start.10 = (f32[38,896]{1,0:T(8,128)S(1)}, f32[38,896]{1,0:T(8,128)}, u32[]{:S(2)}) copy-start(f32[38,896]{1,0:T(8,128)} %get-tuple-element.126) | copy-start | bytes 408580

commit v3 on v2

--- a/solution.py
+++ b/solution.py
@@ -200,6 +200,11 @@
         out[:, pair * 128 : (pair + 1) * 128] = total.astype(BF)
 
 
+def column(row):
+    same = iota((TOK, TOK), 0) == iota((TOK, TOK), 1)
+    return jnp.sum(jnp.where(same, row.astype(F32), 0.0), axis=1, keepdims=True).astype(jnp.int32)
+
+
 def seen_mask(first_key):
     key = iota((TOK, (REACH + 1) * TOK), 1)
     query = REACH * TOK + iota((TOK, 1), 0)
@@ -216,7 +221,7 @@
 
 
 def rotary(pos, freq):
-    angles = pos[...].astype(F32) * freq[...]
+    angles = pos.astype(F32) * freq[...]
     sign = jnp.where(iota((TOK, 128), 1) % 64 < 32, 1.0, -1.0)
     return jnp.cos(angles), jnp.sin(angles) * sign
 
@@ -227,7 +232,7 @@
     return values * cosine + other * sine
 
 
-def forward_kernel(q, kw, v, o, down, gate, up, vec, t, block, pos, freq, *refs):
+def forward_kernel(q, kw, v, o, down, gate, up, qb, vb, g1, g2, t, block, pos, freq, *refs):
     a_out, o_out, do, go, uo, to, mo, seen, qo, att, logs, mid, gains, turn = refs[:14]
     wq, wk, wv, wo, wd, wg, wu, units, own_a, own_o, own_d, own_g, own_u = refs[14:27]
     spread, kv, low, qs, os, ao, oo, send, recv, load, loc = refs[27:]
@@ -256,17 +261,17 @@
     i = iota((32, 28), 1)
     rows28 = where(i + i // 7 == iota((32, 28), 0))
     row = iota((32, 1), 0)
-    i, j = iota((88, 1152), 0), iota((88, 1152), 1)
-    place_at = jnp.where(i < 28, 28 * f + i, jnp.where(i < 32, 1024 + 4 * f + i - 28, -1))
-    extra = jnp.where(row == 7, dot(vec[...], where(place_at == j)), 0.0)
+    i, j = iota((28, D), 0), iota((28, D), 1)
+    entries = where(28 * f + i == j)
+    extra = jnp.where(row == 7, dot(qb[...], entries), 0.0)
+    i, j = iota((4, 128), 0), iota((4, 128), 1)
+    extra_value = jnp.where(row == 7, dot(vb[...], where(4 * f + i == j)), 0.0)
     for copy in loads[:3]:
         copy.wait()
-    own_a[:, :896] = (dot(rows28, wq[...]) + extra[:, :896]).astype(BF)
+    own_a[:, :896] = (dot(rows28, wq[...]) + extra).astype(BF)
     own_a[:, 896:1024] = dot(rows28, wk[...]).astype(BF)
-    own_a[:, 1024:] = (dot(rows28, wv[...]) + extra[:, 1024:]).astype(BF)
-    i, j = iota((88, D), 0), iota((88, D), 1)
-    one = dot(vec[...], where((i >= 32) & (i < 60) & (28 * f + i - 32 == j)))
-    two = dot(vec[...], where((i >= 60) & (28 * f + i - 60 == j)))
+    own_a[:, 1024:] = (dot(rows28, wv[...]) + extra_value).astype(BF)
+    one, two = dot(g1[...], entries), dot(g2[...], entries)
     loads[3].wait()
     own_o[...] = (
         dot(rows28, wo[...]) + jnp.where(row == 7, one, 0.0) + jnp.where(row == 15, two, 0.0)
@@ -342,7 +347,8 @@
         keep(src, out)
     tokens.forward()
     spread[...] = spread_matrix()
-    cosine, sine = rotary(pos, freq)
+    spots = column(pos[...])
+    cosine, sine = rotary(spots, freq)
     turn[0] = cosine
     turn[1] = sine
     for m in range(2):
@@ -388,7 +394,7 @@
         qo[:, some] = turned(qkv[:, some], cosine, -sine).astype(BF)
     spread_heads(qo, qs, 1.0 / math.sqrt(HEAD_SIZE))
     logs[...] = jnp.zeros(logs.shape, F32)
-    first_key = REACH * TOK + iota((TOK, 1), 0) - pos[...]
+    first_key = REACH * TOK + iota((TOK, 1), 0) - spots
     for copy in copies:
         copy.wait_recv()
     for ring in plane:
@@ -432,7 +438,7 @@
     cp.finish()
 
 
-def forward(weights, vec, t, block, pos, freq):
+def forward(weights, vectors, t, block, pos, freq):
     def out(rows, columns):
         return jax.ShapeDtypeStruct((4, 4, 2, rows, columns), BF)
 
@@ -454,7 +460,7 @@
             jax.ShapeDtypeStruct((8, D), F32),
             jax.ShapeDtypeStruct((2, TOK, 128), F32),
         ],
-        in_specs=[HBM] * 7 + [VMEM] + [HBM] + [VMEM] * 3,
+        in_specs=[HBM] * 7 + [VMEM] * 4 + [HBM] + [VMEM] * 3,
         out_specs=[HBM] * 7 + [VMEM] * 7,
         scratch_shapes=[pltpu.VMEM(w.shape, BF) for w in weights]
         + [pltpu.VMEM((2432, 16 * UP), BF)]
@@ -476,7 +482,7 @@
             collective_id=0, has_side_effects=True, vmem_limit_bytes=VMEM_FORWARD
         ),
         name="forward",
-    )(*weights, vec, t, block, pos, freq)
+    )(*weights, *vectors, t, block, pos, freq)
 
 
 def back_kernel(q, grad, att, logs, seen, pos, turn, *refs):
@@ -522,7 +528,7 @@
     spread_heads(q, qs, 1.0 / math.sqrt(HEAD_SIZE))
     spread_heads(grad, gs, 1.0)
     spread_heads(att, os, 1.0)
-    first_key = REACH * TOK + iota((TOK, 1), 0) - pos[...]
+    first_key = REACH * TOK + iota((TOK, 1), 0) - column(pos[...])
     rows = (REACH + 1) * TOK
     grad_keys[...] = jnp.zeros((rows, 128), F32)
     grad_values[...] = jnp.zeros((rows, 128), F32)
@@ -766,7 +772,7 @@
         head, refs = refs[:count], refs[count:]
         return head
 
-    (q_out, k_out, v_out, a_vec, o_out, o_vec, d_out), outs, (t_out,) = take(7), take(n - 1), take(1)
+    (q_out, k_out, v_out, a_vec, o_out, o_vec, d_out), (wide, t_out) = take(7), take(2)
     own, got1, far2, near2, sum2 = (take(2) for _ in range(5))
     line = sum2 + take(n)
     far3, near3, fins, gots = take(2 + n), take(2 + n), take(2 + n), take(2)
@@ -830,6 +836,10 @@
         )
         third[m].plain()
 
+    def columns(m):
+        array, _, first, count, _ = PIECES[m - 2]
+        return pl.ds((array - 1) * UC + first, count)
+
     def close(m):
         third[m].finish()
         total = line[m][x if ways[m] else z].astype(F32)
@@ -839,10 +849,10 @@
             return
         fins[m][...] = total.reshape(fins[m].shape)
         for i in (1, 2, 3):
-            target = gots[m].at[i - 1] if m < 2 else outs[m - 3].at[c]
+            target = gots[m].at[i - 1] if m < 2 else wide.at[c, :, columns(m)]
             closing[m, i] = cp.go(fins[m].at[plus(c, i)], target, ys[i - 1])
         if m > 2:
-            outs[m - 3][c] = fins[m][c]
+            wide[c, :, columns(m)] = fins[m][c]
 
     def join(m, i):
         p = spot(m, i)
@@ -924,7 +934,7 @@
     shapes = pair + [s.shape[1:] for s in sums]
     quarter = [(s[0] // 4, s[1]) for s in shapes]
     outs = [(7, 896), (7, 128), (7, 128), (1, 1152), (7, D), (1, D), (UN, D)]
-    outs += [(4,) + q for q in quarter[3:]]
+    outs += [(4, 8, 2 * UC)]
     scratch = []
     for lead in ((4, 4), (4, 4), (2, 2), (2, 4)):
         scratch += [pltpu.VMEM(lead + s, BF) for s in pair]
@@ -945,7 +955,7 @@
         out_shape=[jax.ShapeDtypeStruct(s, F32) for s in outs]
         + [jax.ShapeDtypeStruct(t.shape[1:], BF)],
         in_specs=[ANY] * (2 + n) + [VMEM] * 2,
-        out_specs=[VMEM] * (7 + n),
+        out_specs=[VMEM] * 9,
         scratch_shapes=scratch,
         compiler_params=pltpu.CompilerParams(
             collective_id=5, has_side_effects=True, vmem_limit_bytes=58 * 1024 * 1024
@@ -1006,7 +1016,7 @@
 
     half = HEAD_SIZE // 2
     frequency = ROTARY_BASE ** (-(np.arange(half) * 2.0 / HEAD_SIZE))
-    places = positions[:, None]
+    places = positions[None]
     (
         all_a,
         all_o,
@@ -1032,7 +1042,7 @@
             gate_weight,
             up_weight,
         ),
-        jnp.concatenate([query_bias, value_bias, first_gain, second_gain])[None],
+        (query_bias[None], value_bias[None], first_gain[None], second_gain[None]),
         cotangent,
         block_input,
         places,
@@ -1087,19 +1097,15 @@
         i896[None, :] // 7 == group, grad_gain_one[None, :], jnp.roll(grad_gain_two, 448)[None, :]
     )
     grad_output_w = jnp.where(jnp.arange(DP)[:, None] % 8 == 7, gains, grad_output_w)
-    sum_q, sum_k, sum_v, vec_a, sum_o, vec_o, sum_d, sum_u0, sum_g, sum_u1, block_output = scatter(
+    sum_q, sum_k, sum_v, vec_a, sum_o, vec_o, sum_d, wide, block_output = scatter(
         grad_qkv_w.astype(BF).reshape(4, 4, 2, 32, 1152),
         grad_output_w.astype(BF).reshape(4, 4, 2, 32, D),
         sums,
         out_part,
         residual_mid,
     )
-    sum_u = jnp.concatenate([sum_u0, sum_u1], axis=2)
-
-    def columns(parts):
-        parts = parts[:, :7].reshape(4, 7, 32, UP)[..., :UN]
-        return jnp.transpose(parts, (1, 2, 0, 3)).reshape(7, FF)
-
+    wide = wide[:, :7].reshape(4, 7, 64, UP)[..., :UN]
+    wide = jnp.transpose(wide, (1, 2, 0, 3)).reshape(7, 2 * FF)
     at = 7 * stretch
     return (
         block_output,
@@ -1112,8 +1118,8 @@
         lax.dynamic_slice(vec_a[0], (1024 + stretch,), (1,)),
         sum_o,
         lax.dynamic_slice(vec_o[0], (lax.rem(at + 448, 896),), (7,)),
-        columns(sum_g),
-        columns(sum_u),
+        wide[:, :FF],
+        wide[:, FF:],
         sum_d,
     )
 

time: 221 us -> 217 us (0.982)
  other arithmetic: 8.08 us -> 5.83 us
where the time goes in v3:
time: 217 us
  Pallas kernels  165 us (76%)
  matrix products  31.4 us (14%)
  local copies, waits for them, and re-layouts  13.1 us (6%)
  other arithmetic  5.83 us (3%)
    pallas_call x1, Pallas kernels, forward(): pl.pallas_call(forward_kernel, out_shape=[out(*p) for p in packed] + [gro...  79.1 us
    pallas_call x1, Pallas kernels, scatter(): pl.pallas_call(scatter_kernel, out_shape=[jax.ShapeDtypeStruct(s, F32) fo...  37.1 us
    pallas_call x1, Pallas kernels, back(): pl.pallas_call(back_kernel, out_shape=[jax.ShapeDtypeStruct((TOK, 1152),...  30.9 us
    pallas_call x1, Pallas kernels, tokens_sum(): pl.pallas_call(tokens_sum_kernel, out_shape=[jax.ShapeDtypeStruct(rows, F...  18.4 us
    dot_general x5, matrix products, dot_t(): lax.dot_general(a, b, (((1,), (1,)), ((), ())), preferred_element_type=F32)  16.9 us
    dot_general x3, matrix products, dot(): return jnp.dot(a, b, preferred_element_type=F32)  8.5 us
    dot_general x2, matrix products, t_dot(): lax.dot_general(a, b, (((0,), (0,)), ((), ())), preferred_element_type=F32)  6.01 us
    unnamed x44, local copies, waits for them, and re-layouts  4.44 us

profile of v3, /device:TPU:0, one launch (start us, length us, event | category | flops | bytes accessed | tf_op | source)
XLA Modules:
  0.0 216.7 jit_solution(12309338040935353009)
XLA Ops:
  0.7 1.1 fusion.29
  1.8 79.1 %forward.1 = (bf16[4,4,2,32,1152]{4,3,2,1,0:T(8,128)(2,1)}, bf16[4,4,2,32,896]{4,3,2,1,0:T(8,128)(2,1)}, bf16[4,4,2,48,896]{4,3,2,1,0:T(8,128)(2,1)}, bf16[4,4,2...) custom-call(bf16[28,896]{1,0:T(8,128)(2,1)} %q.1, ...), custom_call_target="tpu_custom_call" | custom-call | tf_op jit(solution)/shard_map/forward/pallas_call | solution.py:449
  80.9 0.8 slice_reduce_fusion.1
  81.7 0.0 copy-start.16
  81.7 1.3 multiply_reduce_fusion.2
  83.0 2.6 %fusion.12.refs_3_ = bf16[512,1024]{1,0:T(8,128)(2,1)S(1)} fusion(bf16[512,896]{1,0:T(8,128)(2,1)} %bitcast.63, s32[896]{0:T(1024)S(1)} %get-tuple-element.97), kind=kOutput, calls=%fused_computation.20 | convolution fusion | flops 940965888 | bytes 1969664 | tf_op jit(solution)/shard_map/dot_general | solution.py:979
  85.6 0.0 copy-done.16
  85.6 0.0 copy-start.5
  85.6 0.0 copy-start.1
  85.6 0.0 copy-start.6
  85.7 1.8 fusion.56
  87.5 0.3 copy-done.1
  87.8 0.2 copy-done.6
  88.0 1.8 fusion.55
  89.9 0.1 copy-done.15
  89.9 4.1 %multiply_convert_fusion = (bf16[512,1536]{1,0:T(8,128)(2,1)}, bf16[512,1536]{1,0:T(8,128)(2,1)S(1)}, bf16[512,1536]{1,0:T(8,128)(2,1)S(1)}) fusion(f32[512,1536]{1,0:T(8,128)S(1)} %fusion.56, f32[512,1536]{1,0:T(8,128)S(1)} %fusion.55, bf16[512,1024]{1,0:T(8,128)(2,1)S(1)} %fusion.12.refs_3_, bf16[1024,1536]{1,0:T(8,128)(2,1)S(1)} %bitcast.58), kind=kOutput, calls=%fused_computation.9 | convolution fusion | flops 1623195648 | bytes 15204352 | tf_op jit(solution)/shard_map/dot_general | solution.py:979
  94.0 3.2 %fusion.57 = f32[512,1024]{1,0:T(8,128)} fusion(bf16[512,1536]{1,0:T(8,128)(2,1)S(1)} %get-tuple-element.88.refs_4_, bf16[1024,1536]{1,0:T(8,128)(2,1)S(1)} %bitcast.60), kind=kOutput, calls=%fused_computation.90 | convolution fusion | flops 1610612736 | bytes 6815744 | tf_op jit(solution)/shard_map/dot_general | solution.py:983
  97.2 0.0 copy-done.4
  97.2 6.5 %fusion.13 = bf16[512,896]{1,0:T(8,128)(2,1)} fusion(s32[896]{0:T(1024)S(1)} %get-tuple-element.97, f32[512,1024]{1,0:T(8,128)} %fusion.57, bf16[512,1536]{1,0:T(8,128)(2,1)S(1)} %get-tuple-element.89.refs_5_, bf16[1024,1536]{1,0:T(8,128)(2,1)} %bitcast.57), kind=kOutput, calls=%fused_computation.21 | convolution fusion | flops 2552561664 | bytes 7736832 | tf_op jit(solution)/shard_map/dot_general | solution.py:983
  103.7 18.4 %scatter_tokens.1 = (f32[128,896]{1,0:T(8,128)}, bf16[4,128,896]{2,1,0:T(8,128)(2,1)}, bf16[4,4,48,896]{3,2,1,0:T(8,128)(2,1)}, bf16[4,4,32,768]{3,2,1,0:T(8,128...) custom-call(bf16[4,128,896]{2,1,0:T(8,128)(2,1)} %bitcast.49, ...), custom_call_target="tpu_custom_call" | custom-call | tf_op jit(solution)/shard_map/scatter_tokens/pallas_call | solution.py:743
  122.1 0.0 copy-done
  122.1 1.3 multiply_reduce_fusion
  123.4 0.1 fusion.54
  123.5 0.1 pad_maximum_fusion
  123.5 1.2 multiply_add_fusion
  124.8 2.0 fusion.17.grad
  126.8 30.9 %attention_backward.1 = (bf16[128,1152]{1,0:T(8,128)(2,1)}, bf16[4,48,896]{2,1,0:T(8,128)(2,1)}, bf16[4,32,768]{2,1,0:T(8,128)(2,1)}, bf16[4,32,1536]{2,1,0:T(8,128)(2,1)}, bf16[4,32,768]{2,1,0:T(8,128)(2,1)}) custom-call(bf16[128,896]{1,0:T(8,128)(2,1)} %get-tuple-element.48.q, bf16[128,896]{1,0:T(8,128)(2,1)} %fusion.17.grad, ...), custom_call_target="tpu_custom_call" | custom-call | tf_op jit(solution)/shard_map/attention_backward/pallas_call | solution.py:608
  157.7 3.4 %fusion.24 = (f32[128]{0:T(128)S(1)}, bf16[896]{0:T(1024)(128)(2,1)S(1)}, f32[128,896]{1,0:T(8,128)S(1)}) fusion(bf16[128,896]{1,0:T(8,128)(2,1)S(1)} %copy-done.2, f32[896]{0:T(1024)S(1)} %get-tuple-element.85, f32[128]{0:T(128)S(1)} %add_rsqrt_fusion.1, s32[896]{0:T(1024)S(1)} %get-tuple-element.97, bf16[128,1152]{1,0:T(8,128)(2,1)} %get-tuple-element.65, ...), kind=kOutput, calls=%fused_computation.37 | convolution fusion | flops 538721280 | bytes 3352320 | tf_op jit(solution)/shard_map/dot_general | solution.py:983
  161.2 0.9 fusion.28
  162.1 2.9 %select_convert_fusion = bf16[1024,896]{1,0:T(8,128)(2,1)} fusion(bf16[896]{0:T(1024)(128)(2,1)S(1)} %pad_maximum_fusion, bf16[896]{0:T(1024)(128)(2,1)S(1)} %get-tuple-element.84, s32[896]{0:T(1024)S(1)} %get-tuple-element.98, s32[1024]{0:T(1024)S(1)} %add_select_fusion, pred[1024]{0:T(1024)(128)(4,1)S(1)} %fusion.40, bf16[128,896]{1,0:T(8,128)(2,1)S(1)} %copy-done.9, ...), kind=kOutput, calls=%fused_computation.1 | convolution fusion | flops 473677824 | bytes 2539008 | tf_op jit(solution)/shard_map/dot_general | solution.py:987
  164.9 3.1 %convolution_convert_fusion = bf16[1024,1152]{1,0:T(8,128)(2,1)} fusion(bf16[128,1152]{1,0:T(8,128)(2,1)S(1)} %copy-done.18, s32[896]{0:T(1024)S(1)} %get-tuple-element.97, f32[1024]{0:T(1024)S(1)} %fusion.49, bf16[128,896]{1,0:T(8,128)(2,1)S(1)} %copy-done.2, f32[896]{0:T(1024)S(1)} %get-tuple-element.85, f32[128]{0:T(128)S(1)} %add_rsqrt_fusion.1), kind=kOutput, calls=%fused_computation | convolution fusion | flops 539688960 | bytes 2895360 | tf_op jit(solution)/shard_map/dot_general | solution.py:987
  168.1 37.1 %scatter_grads.1 = (f32[7,896]{1,0:T(8,128)}, f32[7,128]{1,0:T(8,128)}, f32[7,128]{1,0:T(8,128)}, f32[1,1152]{1,0:T(1,128)}, f32[7,896]{1,0:T(8,128)}, /*index=5...) custom-call(bf16[4,4,2,32,1152]{4,3,2,1,0:T(8,128)(2,1)} %bitcast.45, ...), custom_call_target="tpu_custom_call" | custom-call | tf_op jit(solution)/shard_map/scatter_grads/pallas_call | solution.py:953
  205.1 1.3 constant_dynamic-slice_fusion.1
  206.4 1.2 fusion.51
  207.6 1.3 fusion.52
  208.9 1.2 copy.29
  210.1 0.4 reshape.205
  210.6 0.1 slice_bitcast_fusion
  210.7 0.6 copy.30
  211.3 0.9 reshape.206
  212.2 0.7 fusion.53
  213.0 0.7 copy.37
  213.7 0.6 copy.38
  214.3 0.6 copy.39
  214.9 0.0 copy-done.13
  214.9 0.6 copy.40
  215.5 0.6 copy.41
  216.1 0.7 copy.42
  (35 shorter events, 0.1 us)
Async XLA Ops:
  81.7 3.9 %copy-start.16 = (bf16[4,4,2,32,1536]{4,3,2,1,0:T(8,128)(2,1)S(1)}, bf16[4,4,2,32,1536]{4,3,2,1,0:T(8,128)(2,1)}, u32[]{:S(2)}) copy-start(bf16[4,4,2,32,1536]{4,3,2,1,0:T(8,128)(2,1)} %get-tuple-element.54) | copy-start | bytes 9437188
  85.6 4.2 %copy-start.5 = (bf16[512,1024]{1,0:T(8,128)(2,1)}, bf16[512,1024]{1,0:T(8,128)(2,1)S(1)}, u32[]{:S(2)}) copy-start(bf16[512,1024]{1,0:T(8,128)(2,1)S(1)} %fusion.12.refs_3_) | copy-start | bytes 3145732
  85.6 2.2 copy-start.1
  85.6 2.4 %copy-start.6 = (bf16[4,128,896]{2,1,0:T(8,128)(2,1)S(1)}, bf16[4,128,896]{2,1,0:T(8,128)(2,1)}, u32[]{:S(2)}) copy-start(bf16[4,128,896]{2,1,0:T(8,128)(2,1)} %get-tuple-element.50) | copy-start | bytes 2752516
  88.0 1.9 copy-start.15
  94.0 3.2 %copy-start.3 = (bf16[512,1536]{1,0:T(8,128)(2,1)}, bf16[512,1536]{1,0:T(8,128)(2,1)S(1)}, u32[]{:S(2)}) copy-start(bf16[512,1536]{1,0:T(8,128)(2,1)S(1)} %get-tuple-element.88.refs_4_) | copy-start | bytes 4718596
  94.0 3.2 %copy-start.4 = (bf16[512,1536]{1,0:T(8,128)(2,1)}, bf16[512,1536]{1,0:T(8,128)(2,1)S(1)}, u32[]{:S(2)}) copy-start(bf16[512,1536]{1,0:T(8,128)(2,1)S(1)} %get-tuple-element.89.refs_5_) | copy-start | bytes 4718596
  103.7 18.4 %copy-start = (f32[128,896]{1,0:T(8,128)S(1)}, f32[128,896]{1,0:T(8,128)}, u32[]{:S(2)}) copy-start(f32[128,896]{1,0:T(8,128)} %get-tuple-element.49.mid) | copy-start | bytes 1376260
  103.7 19.9 %copy-start.7 = (bf16[128,896]{1,0:T(8,128)(2,1)S(1)}, bf16[128,896]{1,0:T(8,128)(2,1)}, u32[]{:S(2)}) copy-start(bf16[128,896]{1,0:T(8,128)(2,1)} %t.1) | copy-start | bytes 688132
  103.7 21.1 %copy-start.17 = (bf16[4,4,2,32,896]{4,3,2,1,0:T(8,128)(2,1)S(1)}, bf16[4,4,2,32,896]{4,3,2,1,0:T(8,128)(2,1)}, u32[]{:S(2)}) copy-start(bf16[4,4,2,32,896]{4,3,2,1,0:T(8,128)(2,1)} %get-tuple-element.56) | copy-start | bytes 5505028
  126.8 31.0 %copy-start.2 = (bf16[128,896]{1,0:T(8,128)(2,1)S(1)}, bf16[128,896]{1,0:T(8,128)(2,1)}, u32[]{:S(2)}) copy-start(bf16[128,896]{1,0:T(8,128)(2,1)} %block.1) | copy-start | bytes 688132
  157.7 4.3 %copy-start.9 = (bf16[128,896]{1,0:T(8,128)(2,1)S(1)}, bf16[128,896]{1,0:T(8,128)(2,1)}, u32[]{:S(2)}) copy-start(bf16[128,896]{1,0:T(8,128)(2,1)} %get-tuple-element.57.att) | copy-start | bytes 688132
  162.0 2.9 %copy-start.18 = (bf16[128,1152]{1,0:T(8,128)(2,1)S(1)}, bf16[128,1152]{1,0:T(8,128)(2,1)}, u32[]{:S(2)}) copy-start(bf16[128,1152]{1,0:T(8,128)(2,1)} %get-tuple-element.65) | copy-start | bytes 884740
  210.1 2.9 %copy-start.8 = (bf16[128,896]{1,0:T(8,128)(2,1)S(1)}, bf16[128,896]{1,0:T(8,128)(2,1)}, u32[]{:S(2)}) copy-start(bf16[128,896]{1,0:T(8,128)(2,1)} %get-tuple-element.112) | copy-start | bytes 688132
  210.6 3.1 %copy-start.12 = (f32[7,896]{1,0:T(8,128)S(1)}, f32[7,896]{1,0:T(8,128)}, u32[]{:S(2)}) copy-start(f32[7,896]{1,0:T(8,128)} %get-tuple-element.115) | copy-start | bytes 75268
  210.6 3.7 %copy-start.14 = (f32[7,128]{1,0:T(8,128)S(1)}, f32[7,128]{1,0:T(8,128)}, u32[]{:S(2)}) copy-start(f32[7,128]{1,0:T(8,128)} %get-tuple-element.117) | copy-start | bytes 10756
  210.6 4.3 %copy-start.13 = (f32[7,128]{1,0:T(8,128)S(1)}, f32[7,128]{1,0:T(8,128)}, u32[]{:S(2)}) copy-start(f32[7,128]{1,0:T(8,128)} %get-tuple-element.118) | copy-start | bytes 10756
  210.6 4.9 %copy-start.11 = (f32[7,896]{1,0:T(8,128)S(1)}, f32[7,896]{1,0:T(8,128)}, u32[]{:S(2)}) copy-start(f32[7,896]{1,0:T(8,128)} %get-tuple-element.120) | copy-start | bytes 75268
  210.6 5.5 %copy-start.10 = (f32[38,896]{1,0:T(8,128)S(1)}, f32[38,896]{1,0:T(8,128)}, u32[]{:S(2)}) copy-start(f32[38,896]{1,0:T(8,128)} %get-tuple-element.124) | copy-start | bytes 408580
